TPU v7x, 32 devices: a whole 2x2x4 slice. The times are simulated.
32 devices in a mesh: fsdp: 16 (over z, x, core), tp: 2 (over y).
Axes of the slice: x: 2, y: 2, z: 4, core: 2. Of those that a mesh axis runs over, the one named last changes fastest.
Arguments:
- tokens: bfloat16 [64, 256, 768], P('fsdp', 'tp'), may hold values from -6 to 6
- cotangent: bfloat16 [64, 256, 768], P('fsdp', 'tp'), may hold values from -6 to 6
- image_counts: int32 [16], P('fsdp'), may hold values from 2 to 4, as said below
- split_points: int32 [64], P('fsdp'), may hold values from 69 to 128, as said below
- attend_gain: bfloat16 [768], P('fsdp'), may hold values from 0.5 to 1.5
- attend_shift: bfloat16 [768], P('fsdp'), may hold values from -3 to 3
- qkv_weight: bfloat16 [768, 3, 768], P('fsdp', None, 'tp'), may hold values from -0.21875 to 0.21875
- query_value_bias: bfloat16 [2, 768], P(None, ('tp', 'fsdp')), may hold values from -3 to 3
- output_weight: bfloat16 [768, 768], P('tp', 'fsdp'), may hold values from -0.875 to 0.875
- output_bias: bfloat16 [768], P('fsdp'), may hold values from -3 to 3
- dense_gain: bfloat16 [768], P('fsdp'), may hold values from 0.5 to 1.5
- dense_shift: bfloat16 [768], P('fsdp'), may hold values from -3 to 3
- up_weight: bfloat16 [768, 3072], P('fsdp', 'tp'), may hold values from -0.21875 to 0.21875
- up_bias: bfloat16 [3072], P(('tp', 'fsdp')), may hold values from -3 to 3
- down_weight: bfloat16 [3072, 768], P('tp', 'fsdp'), may hold values from -0.109375 to 0.109375
- down_bias: bfloat16 [768], P('fsdp'), may hold values from -3 to 3
Outputs:
- out_tokens: bfloat16 [64, 256, 768], P('fsdp', 'tp')
- grad_tokens: float32 [64, 256, 768], P('fsdp', 'tp')
- grad_attend_gain: float32 [768], P('fsdp')
- grad_attend_shift: float32 [768], P('fsdp')
- grad_qkv_weight: float32 [768, 3, 768], P('fsdp', None, 'tp')
- grad_query_value_bias: float32 [2, 768], P(None, ('tp', 'fsdp'))
- grad_output_weight: float32 [768, 768], P('tp', 'fsdp')
- grad_output_bias: float32 [768], P('fsdp')
- grad_dense_gain: float32 [768], P('fsdp')
- grad_dense_shift: float32 [768], P('fsdp')
- grad_up_weight: float32 [768, 3072], P('fsdp', 'tp')
- grad_up_bias: float32 [3072], P(('tp', 'fsdp'))
- grad_down_weight: float32 [3072, 768], P('tp', 'fsdp')
- grad_down_bias: float32 [768], P('fsdp')
Inputs may be any that keep to these rules, and one draw needn't show every extreme that they name: image_counts[f] live images fill the first image slots of fsdp index f; some index has all 4 live. `split_points`: some image has 128 tokens in its first half and some has 69.
All inputs are finite; a program needn't handle non-finite values.
Results may differ from a plain program's by a relative error of at most 0.015.
Values may be sent and summed in bfloat16 or wider, within the bound.
No kernel may reach another device: no remote copies, remote signals or barrier semaphores. Data moves between devices by JAX's collectives and lax.ppermute only.
A program may use at most 128 MiB of HBM per device.

v0:
```python
from functools import partial

import jax
import jax.numpy as jnp
from jax import lax
from jax.sharding import PartitionSpec as P

HD = 64
SEQ = 197


norm_epsilon = 1e-06
masked_score = -1e30


def normalize(values, norm_gain, norm_shift):
    centre = values - jnp.mean(values, axis=-1, keepdims=True)
    spread = jnp.mean(centre * centre, axis=-1, keepdims=True)
    return centre * lax.rsqrt(spread + norm_epsilon) * norm_gain + norm_shift


def paired(array):
    return array.reshape((array.shape[0] // 2, 2) + array.shape[1:])


def unpaired(array):
    return array.reshape((array.shape[0] * 2,) + array.shape[2:])


def block_scores(query_rows, key_rows, keys_live, scaling):
    scores = (
        jnp.einsum("bqhe,bkhe->bhqk", query_rows, key_rows, preferred_element_type=jnp.float32)
        * scaling
    )
    return jnp.where(keys_live[:, None, None, :], scores, masked_score)


def attend_forward(query_rows, key_rows, value_rows, keys_live, scaling):
    scores = block_scores(query_rows, key_rows, keys_live, scaling)
    row_top = jnp.max(scores, axis=-1, keepdims=True)
    raised = jnp.exp(scores - row_top)
    row_total = jnp.sum(raised, axis=-1, keepdims=True)
    chances = (raised / row_total).astype(jnp.bfloat16)
    mixed = jnp.einsum("bhqk,bkhe->bqhe", chances, value_rows, preferred_element_type=jnp.float32)
    return (mixed.astype(jnp.bfloat16), (row_top + jnp.log(row_total))[..., 0])


def attend_backward(query_rows, key_rows, value_rows, keys_live, log_total, grad_mixed, scaling):
    scores = block_scores(query_rows, key_rows, keys_live, scaling)
    chances = jnp.exp(scores - log_total[..., None])
    rounded = chances.astype(jnp.bfloat16)
    grad_value = jnp.einsum(
        "bhqk,bqhe->bkhe", rounded, grad_mixed, preferred_element_type=jnp.float32
    )
    grad_chance = jnp.einsum(
        "bqhe,bkhe->bhqk", grad_mixed, value_rows, preferred_element_type=jnp.float32
    )
    centred = grad_chance - jnp.sum(chances * grad_chance, axis=-1, keepdims=True)
    grad_scores = (chances * centred).astype(jnp.bfloat16)
    grad_query = (
        jnp.einsum("bhqk,bkhe->bqhe", grad_scores, key_rows, preferred_element_type=jnp.float32)
        * scaling
    )
    grad_key = (
        jnp.einsum("bhqk,bqhe->bkhe", grad_scores, query_rows, preferred_element_type=jnp.float32)
        * scaling
    )
    return (
        grad_query.astype(jnp.bfloat16),
        grad_key.astype(jnp.bfloat16),
        grad_value.astype(jnp.bfloat16),
    )


def gather_attend(pieces):
    return (
        lax.all_gather(pieces[0], "fsdp", axis=0, tiled=True),
        lax.all_gather(pieces[1], "fsdp", axis=0, tiled=True),
        lax.all_gather(pieces[2], "fsdp", axis=0, tiled=True),
        lax.all_gather(pieces[3], "fsdp", axis=1, tiled=True),
        lax.all_gather(pieces[4], "fsdp", axis=1, tiled=True),
        lax.all_gather(pieces[5], "fsdp", axis=0, tiled=True),
    )


def gather_dense(pieces):
    return (
        lax.all_gather(pieces[0], "fsdp", axis=0, tiled=True),
        lax.all_gather(pieces[1], "fsdp", axis=0, tiled=True),
        lax.all_gather(pieces[2], "fsdp", axis=0, tiled=True),
        lax.all_gather(pieces[3], "fsdp", axis=0, tiled=True),
        lax.all_gather(pieces[4], "fsdp", axis=1, tiled=True),
        lax.all_gather(pieces[5], "fsdp", axis=0, tiled=True),
    )


def spread_rows(values):
    return lax.all_gather(values, "tp", axis=1, tiled=True)


def fold_rows(values):
    return lax.psum_scatter(
        values.astype(jnp.bfloat16), "tp", scatter_dimension=1, tiled=True
    ).astype(jnp.float32)


def spread_grads(values):
    return lax.all_gather(values, "tp", axis=1, tiled=True)


def fold_grads(values):
    return lax.psum_scatter(
        values.astype(jnp.bfloat16), "tp", scatter_dimension=1, tiled=True
    ).astype(jnp.float32)


def tp_total(values):
    return lax.psum(values, "tp")


def on_device(
    tokens,
    cotangent,
    image_counts,
    split_points,
    attend_gain,
    attend_shift,
    qkv_weight,
    query_value_bias,
    output_weight,
    output_bias,
    dense_gain,
    dense_shift,
    up_weight,
    up_bias,
    down_weight,
    down_bias,
):
    images, slot_count, width = tokens.shape
    half_index = lax.axis_index("tp")
    scaling = HD ** (-0.5)
    place = jnp.arange(slot_count)
    upper_bound = SEQ - split_points
    own_bound = jnp.where(half_index == 0, split_points, upper_bound)
    live_images = jnp.arange(images) < image_counts[0]
    row_live = (live_images[:, None] & (place[None, :] < own_bound[:, None])).astype(jnp.float32)[
        :, :, None
    ]
    keys_live = jnp.concatenate(
        [place[None, :] < split_points[:, None], place[None, :] < upper_bound[:, None]], axis=1
    )
    attend_set = gather_attend(
        (attend_gain, attend_shift, qkv_weight, query_value_bias, output_weight, output_bias)
    )
    first_gain, first_shift, joint_weight, joint_bias, output_matrix, output_add = attend_set
    inputs = tokens.astype(jnp.float32)
    first_gain_wide = first_gain.astype(jnp.float32)
    first_shift_wide = first_shift.astype(jnp.float32)
    normed_one = normalize(inputs, first_gain_wide, first_shift_wide).astype(jnp.bfloat16)
    first_rows = spread_rows(normed_one)
    joint = jnp.einsum(
        "gsd,dcn->gscn", first_rows, joint_weight, preferred_element_type=jnp.float32
    )
    bias_wide = joint_bias.astype(jnp.float32)
    heads_here = joint.shape[-1] // HD
    full_length = 2 * slot_count
    head_shape = (images, full_length, heads_here, HD)
    query_rows = (joint[:, :, 0] + bias_wide[0]).astype(jnp.bfloat16).reshape(head_shape)
    key_rows = joint[:, :, 1].astype(jnp.bfloat16).reshape(head_shape)
    value_rows = (joint[:, :, 2] + bias_wide[1]).astype(jnp.bfloat16).reshape(head_shape)
    mixed, log_total = lax.map(
        lambda blocks: attend_forward(blocks[0], blocks[1], blocks[2], blocks[3], scaling),
        (paired(query_rows), paired(key_rows), paired(value_rows), paired(keys_live)),
    )
    mixed = unpaired(mixed).reshape(images, full_length, heads_here * HD)
    log_total = unpaired(log_total)
    branch = fold_rows(
        jnp.einsum("gsn,nd->gsd", mixed, output_matrix, preferred_element_type=jnp.float32)
    )
    middle = inputs + branch + output_add.astype(jnp.float32)
    dense_set = gather_dense((dense_gain, dense_shift, up_weight, up_bias, down_weight, down_bias))
    second_gain, second_shift, upward_matrix, upward_add, downward_matrix, downward_add = dense_set
    normed_two = normalize(
        middle, second_gain.astype(jnp.float32), second_shift.astype(jnp.float32)
    ).astype(jnp.bfloat16)
    second_rows = spread_rows(normed_two)
    hidden = jnp.einsum(
        "gsd,df->gsf", second_rows, upward_matrix, preferred_element_type=jnp.float32
    ) + upward_add.astype(jnp.float32)
    active = jax.nn.gelu(hidden, approximate=False).astype(jnp.bfloat16)
    dense_out = fold_rows(
        jnp.einsum("gsf,fd->gsd", active, downward_matrix, preferred_element_type=jnp.float32)
    )
    result = middle + dense_out + downward_add.astype(jnp.float32)
    out_tokens = (result * row_live).astype(jnp.bfloat16)
    back_dense = (
        lax.all_gather(dense_gain, "fsdp", axis=0, tiled=True),
        lax.all_gather(dense_shift, "fsdp", axis=0, tiled=True),
        lax.all_gather(up_weight, "fsdp", axis=0, tiled=True),
        lax.all_gather(up_bias, "fsdp", axis=0, tiled=True),
        lax.all_gather(down_weight, "fsdp", axis=1, tiled=True),
        lax.all_gather(down_bias, "fsdp", axis=0, tiled=True),
    )
    back_attend = (
        lax.all_gather(attend_gain, "fsdp", axis=0, tiled=True),
        lax.all_gather(attend_shift, "fsdp", axis=0, tiled=True),
        lax.all_gather(qkv_weight, "fsdp", axis=0, tiled=True),
        lax.all_gather(query_value_bias, "fsdp", axis=1, tiled=True),
        lax.all_gather(output_weight, "fsdp", axis=1, tiled=True),
        lax.all_gather(output_bias, "fsdp", axis=0, tiled=True),
    )
    second_gain, second_shift, upward_matrix, upward_add, downward_matrix, downward_add = back_dense
    grad_out = cotangent.astype(jnp.float32) * row_live
    grad_down_in = spread_grads(grad_out.astype(jnp.bfloat16))
    grad_downward = jnp.einsum(
        "gsf,gsd->fd", active, grad_down_in, preferred_element_type=jnp.float32
    )
    grad_active = jnp.einsum(
        "gsd,fd->gsf", grad_down_in, downward_matrix, preferred_element_type=jnp.float32
    )
    unused_gelu, gelu_back = jax.vjp(partial(jax.nn.gelu, approximate=False), hidden)
    grad_hidden = gelu_back(grad_active)[0].astype(jnp.bfloat16)
    grad_upward = jnp.einsum(
        "gsd,gsf->df", second_rows, grad_hidden, preferred_element_type=jnp.float32
    )
    grad_upward_add = jnp.sum(grad_hidden, axis=(0, 1), dtype=jnp.float32)
    grad_second = fold_grads(
        jnp.einsum("gsf,df->gsd", grad_hidden, upward_matrix, preferred_element_type=jnp.float32)
    )
    unused_second, second_back = jax.vjp(
        normalize, middle, second_gain.astype(jnp.float32), second_shift.astype(jnp.float32)
    )
    grad_middle_norm, grad_second_gain, grad_second_shift = second_back(grad_second)
    grad_middle = grad_out + grad_middle_norm
    small_second = tp_total(
        jnp.stack([grad_second_gain, grad_second_shift, jnp.sum(grad_out, axis=(0, 1))])
    )
    dense_grads = (
        lax.psum_scatter(small_second[0], "fsdp", scatter_dimension=0, tiled=True),
        lax.psum_scatter(small_second[1], "fsdp", scatter_dimension=0, tiled=True),
        lax.psum_scatter(grad_upward, "fsdp", scatter_dimension=0, tiled=True),
        lax.psum_scatter(grad_upward_add, "fsdp", scatter_dimension=0, tiled=True),
        lax.psum_scatter(grad_downward, "fsdp", scatter_dimension=1, tiled=True),
        lax.psum_scatter(small_second[2], "fsdp", scatter_dimension=0, tiled=True),
    )
    first_gain, first_shift, joint_weight, joint_bias, output_matrix, output_add = back_attend
    grad_branch = spread_grads(grad_middle.astype(jnp.bfloat16))
    grad_output_matrix = jnp.einsum(
        "gsn,gsd->nd", mixed, grad_branch, preferred_element_type=jnp.float32
    )
    grad_mixed = jnp.einsum(
        "gsd,nd->gsn", grad_branch, output_matrix, preferred_element_type=jnp.float32
    )
    grad_mixed = grad_mixed.astype(jnp.bfloat16).reshape(head_shape)
    grad_query, grad_key, grad_value = lax.map(
        lambda blocks: attend_backward(
            blocks[0], blocks[1], blocks[2], blocks[3], blocks[4], blocks[5], scaling
        ),
        (
            paired(query_rows),
            paired(key_rows),
            paired(value_rows),
            paired(keys_live),
            paired(log_total),
            paired(grad_mixed),
        ),
    )
    grad_joint = jnp.stack([unpaired(grad_query), unpaired(grad_key), unpaired(grad_value)], axis=2)
    grad_joint = grad_joint.reshape(images, full_length, 3, heads_here * HD)
    grad_joint_weight = jnp.einsum(
        "gsd,gscn->dcn", first_rows, grad_joint, preferred_element_type=jnp.float32
    )
    grad_joint_bias = jnp.sum(grad_joint[:, :, 0::2], axis=(0, 1), dtype=jnp.float32)
    grad_first = fold_grads(
        jnp.einsum("gscn,dcn->gsd", grad_joint, joint_weight, preferred_element_type=jnp.float32)
    )
    unused_first, first_back = jax.vjp(
        normalize, inputs, first_gain.astype(jnp.float32), first_shift.astype(jnp.float32)
    )
    grad_inputs_norm, grad_first_gain, grad_first_shift = first_back(grad_first)
    grad_tokens = grad_middle + grad_inputs_norm
    small_first = tp_total(
        jnp.stack([grad_first_gain, grad_first_shift, jnp.sum(grad_middle, axis=(0, 1))])
    )
    attend_grads = (
        lax.psum_scatter(small_first[0], "fsdp", scatter_dimension=0, tiled=True),
        lax.psum_scatter(small_first[1], "fsdp", scatter_dimension=0, tiled=True),
        lax.psum_scatter(grad_joint_weight, "fsdp", scatter_dimension=0, tiled=True),
        lax.psum_scatter(grad_joint_bias, "fsdp", scatter_dimension=1, tiled=True),
        lax.psum_scatter(grad_output_matrix, "fsdp", scatter_dimension=1, tiled=True),
        lax.psum_scatter(small_first[2], "fsdp", scatter_dimension=0, tiled=True),
    )
    return (
        out_tokens,
        grad_tokens,
        attend_grads[0],
        attend_grads[1],
        attend_grads[2],
        attend_grads[3],
        attend_grads[4],
        attend_grads[5],
        dense_grads[0],
        dense_grads[1],
        dense_grads[2],
        dense_grads[3],
        dense_grads[4],
        dense_grads[5],
    )


def solution(mesh):
    return jax.shard_map(
        on_device,
        mesh=mesh,
        in_specs=(
            P("fsdp", "tp", None),
            P("fsdp", "tp", None),
            P("fsdp"),
            P("fsdp"),
            P("fsdp"),
            P("fsdp"),
            P("fsdp", None, "tp"),
            P(None, ("tp", "fsdp")),
            P("tp", "fsdp"),
            P("fsdp"),
            P("fsdp"),
            P("fsdp"),
            P("fsdp", "tp"),
            P(("tp", "fsdp")),
            P("tp", "fsdp"),
            P("fsdp"),
        ),
        out_specs=(
            P("fsdp", "tp", None),
            P("fsdp", "tp", None),
            P("fsdp"),
            P("fsdp"),
            P("fsdp", None, "tp"),
            P(None, ("tp", "fsdp")),
            P("tp", "fsdp"),
            P("fsdp"),
            P("fsdp"),
            P("fsdp"),
            P("fsdp", "tp"),
            P(("tp", "fsdp")),
            P("tp", "fsdp"),
            P("fsdp"),
        ),
        check_vma=False,
    )
```

profile of v0, /device:TPU:0, one launch (start us, length us, event | category | flops | bytes accessed | tf_op | source)
XLA Modules:
  0.0 807.5 jit_solution(3934712669728813721)
XLA Ops:
  15.7 62.9 %all-reduce.17 = (bf16[768]{0:T(1024)(128)(2,1)S(1)}, bf16[768]{0:T(1024)(128)(2,1)S(1)}, bf16[768]{0:T(1024)(128)(2,1)S(1)}, bf16[768]{0:T(1024)(128)(2,1)S(1)}...) all-reduce(bf16[768]{0:T(1024)(128)(2,1)S(1)} %dynamic-update-slice, ...), channel_id=1, replica_groups=mesh['fsdp'=16,'tp'=2] {'fsdp'}, use_global_device_ids=true, to_apply=%add.4 | all-reduce | flops 6144 | bytes 24576
  83.7 17.0 %all-gather = bf16[16,24,2]{1,2,0:T(2,128)(2,1)S(1)} all-gather(bf16[1,24,2]{1,2,0:T(2,128)(2,1)S(1)} %bitcast.201), channel_id=1, replica_groups=mesh['fsdp'=16,'tp'=2] {'fsdp'}, dimensions={0}, use_global_device_ids=true | all-gather | bytes 1632 | tf_op jit(solution)/shard_map/all_gather | solution.py:80
  101.3 22.2 %all_gather.59 = bf16[384,768]{0,1:T(8,128)(2,1)} all-gather(bf16[384,48]{0,1:T(8,128)(2,1)S(1)} %copy-done.19), channel_id=1, replica_groups=mesh['fsdp'=16,'tp'=2] {'fsdp'}, dimensions={1}, use_global_device_ids=true | all-gather | bytes 626688 | tf_op jit(solution)/shard_map/all_gather | solution.py:81
  123.4 26.8 %all-gather.11.cloned.1.call-done = bf16[768,3,384]{2,0,1:T(8,128)(2,1)} async-done(((bf16[48,3,384]{2,0,1:T(8,128)(2,1)}), bf16[768,3,384]{2,0,1:T(8,128)(2,1)}) %all-gather.11.cloned.1.call-update) | async-done | bytes 1769488 | tf_op jit(solution)/shard_map/all_gather | solution.py:79
  150.2 4.2 fusion.76
  164.0 6.5 while.26
  170.4 3.7 convolution_convert_fusion
  174.8 24.5 %reduce-scatter.10.cloned.1.call-done = bf16[4,128,768]{2,1,0:T(8,128)(2,1)} async-done(((bf16[4,256,768]{2,1,0:T(8,128)(2,1)}), bf16[4,128,768]{2,1,0:T(8,128)(2,1)}) %reduce-scatter.10.cloned.1.call-update) | async-done | bytes 786448 | tf_op jit(solution)/shard_map/reduce_scatter | solution.py:102
  206.7 37.4 %all-gather.15.cloned.1.call-done = bf16[768,1536]{1,0:T(8,128)(2,1)} async-done(((bf16[48,1536]{1,0:T(8,128)(2,1)}), bf16[768,1536]{1,0:T(8,128)(2,1)}) %all-gather.15.cloned.1.call-update) | async-done | bytes 2359312 | tf_op jit(solution)/shard_map/all_gather | solution.py:90
  244.1 28.1 %all-gather.13.cloned.1.call-done = bf16[4,256,768]{2,1,0:T(8,128)(2,1)} async-done(((bf16[4,128,768]{2,1,0:T(8,128)(2,1)}), bf16[4,256,768]{2,1,0:T(8,128)(2,1)}) %all-gather.13.cloned.1.call-update) | async-done | bytes 1572880 | tf_op jit(solution)/shard_map/all_gather | solution.py:98
  272.2 6.2 fusion.97
  281.0 15.6 %multiply_convert_fusion.1 = (bf16[4,256,1536]{2,1,0:T(8,128)(2,1)}, f32[4,256,1536]{2,1,0:T(8,128)}) fusion(f32[4,256,1536]{2,1,0:T(8,128)S(1)} %get-tuple-element.212, f32[1536]{0:T(1024)S(1)} %convert_element_type.153, u8[256,1536]{1,0:T(8,128)(4,1)S(1)} %get-tuple-element.129, u8[256,1536]{1,0:T(8,128)(4,1)S(1)} %get-tuple-element.128), kind=kLoop, calls=%fused_computation.69 | loop fusion | flops 111673344 | bytes 16521216 | tf_op jit(solution)/shard_map/convert_element_type | solution.py:190
  296.6 4.9 all-gather.19.cloned.1.call-done
  301.5 44.9 %all-gather.17.cloned.1.call-done = bf16[1536,768]{0,1:T(8,128)(2,1)} async-done(((bf16[1536,48]{0,1:T(8,128)(2,1)}), bf16[1536,768]{0,1:T(8,128)(2,1)}) %all-gather.17.cloned.1.call-update) | async-done | bytes 2359312 | tf_op jit(solution)/shard_map/all_gather | solution.py:92
  346.3 10.4 %convert_reduce_fusion = (f32[1536]{0:T(1024)S(1)}, bf16[4,256,1536]{2,1,0:T(8,128)(2,1)S(1)}) fusion(f32[4,256,1536]{2,1,0:T(8,128)} %get-tuple-element.199, bf16[4,256,768]{2,1,0:T(8,128)(2,1)} %all-gather.19.cloned.1.call-done, bf16[1536,768]{0,1:T(8,128)(2,1)} %all-gather.17.cloned.1.call-done, f32[4,256,1536]{2,1,0:T(8,128)} %copy-done.9, ...), kind=kOutput, calls=%fused_computation.67 | convolution fusion | flops 2442656256 | bytes 19673088 | tf_op jit(solution)/shard_map/gsd,fd->gsf/dot_general | solution.py:218
  358.4 3.7 fusion.78
  362.2 25.0 %reduce-scatter.14.cloned.1.call-done = bf16[4,128,768]{2,1,0:T(8,128)(2,1)} async-done(((bf16[4,256,768]{2,1,0:T(8,128)(2,1)}), bf16[4,128,768]{2,1,0:T(8,128)(2,1)}) %reduce-scatter.14.cloned.1.call-update) | async-done | bytes 786448 | tf_op jit(solution)/shard_map/reduce_scatter | solution.py:112
  392.0 27.1 %all-gather.21.cloned.1.call-done = bf16[4,256,768]{2,1,0:T(8,128)(2,1)} async-done(((bf16[4,128,768]{2,1,0:T(8,128)(2,1)}), bf16[4,256,768]{2,1,0:T(8,128)(2,1)}) %all-gather.21.cloned.1.call-update) | async-done | bytes 1572880 | tf_op jit(solution)/shard_map/all_gather | solution.py:108
  419.2 3.4 convolution_convert_fusion.1
  427.7 15.2 %while.27 = (s32[]{:T(128)}, bf16[2,2,256,6,64]{2,4,3,1,0:T(8,128)(2,1)}, bf16[2,2,256,6,64]{2,4,3,1,0:T(8,128)(2,1)}, bf16[2,2,256,6,64]{2,4,3,1,0:T(8,128)(2,1...) while((s32[]{:T(128)}, ...), condition=%wide.region_15.16_spmd, body=%wide.region_13.15_spmd.sunk | while | flops 511374336 | bytes 43326720 | solution.py:255
  448.2 5.1 bitcast_convert_fusion
  453.4 6.4 fusion.81
  459.9 3.7 convolution_bitcast_fusion.3
  463.7 7.1 convolution_bitcast_fusion.1
  471.1 7.2 convolution_bitcast_fusion
  478.4 5.7 convolution_bitcast_fusion.2
  492.3 8.0 all-reduce.16
  500.3 60.3 %all-reduce.15 = (f32[768]{0:T(1024)S(1)}, f32[768]{0:T(1024)S(1)}, f32[2,384]{1,0:T(2,128)S(1)}, f32[768]{0:T(1024)S(1)}, f32[768]{0:T(1024)S(1)}, /*index=5*/f...) all-reduce(f32[768]{0:T(1024)S(1)} %get-tuple-element.144, ...), channel_id=6, replica_groups=mesh['fsdp'=16,'tp'=2] {'fsdp'}, use_global_device_ids=true, to_apply=%region_23.24.clone | all-reduce | flops 6912 | bytes 55296
  565.4 3.8 add_add_fusion.2
  570.8 79.0 %reduce-scatter.22.cloned.1.call-done = f32[48,1536]{1,0:T(8,128)} async-done(((f32[768,1536]{1,0:T(8,128)}), f32[48,1536]{1,0:T(8,128)}) %reduce-scatter.22.cloned.1.call-update) | async-done | bytes 294928 | tf_op jit(solution)/shard_map/reduce_scatter | solution.py:241
  649.8 79.4 %reduce-scatter.24.cloned.1.call-done = f32[1536,48]{0,1:T(8,128)} async-done(((f32[1536,768]{0,1:T(8,128)}), f32[1536,48]{0,1:T(8,128)}) %reduce-scatter.24.cloned.1.call-update) | async-done | bytes 294928 | tf_op jit(solution)/shard_map/reduce_scatter | solution.py:243
  729.1 71.4 %reduce-scatter.18.cloned.1.call-done = f32[48,3,384]{2,0,1:T(8,128)} async-done(((f32[768,3,384]{2,0,1:T(8,128)}), f32[48,3,384]{2,0,1:T(8,128)}) %reduce-scatter.18.cloned.1.call-update) | async-done | bytes 221200 | tf_op jit(solution)/shard_map/reduce_scatter | solution.py:288
  (215 shorter events, 83.6 us)
Async XLA Ops:
  7.2 74.4 %copy-start = (bf16[4,128,768]{2,1,0:T(8,128)(2,1)S(1)}, bf16[4,128,768]{2,1,0:T(8,128)(2,1)}, u32[]{:S(2)}) copy-start(bf16[4,128,768]{2,1,0:T(8,128)(2,1)} %param.20) | copy-start | bytes 2359300
  7.2 116.2 %all-gather.9.cloned.1.call-start = ((), (), s32[]{:S(2)}) async-start(), calls=%async_computation.8 | async-start | bytes 2359296 | tf_op jit(solution)/shard_map/all_gather | solution.py:98
  78.7 4.2 copy-start.15
  80.0 3.7 copy-start.25
  80.0 21.0 %copy-start.26 = (s32[4]{0:T(128)S(1)}, s32[4]{0:T(128)}, u32[]{:S(2)}) copy-start(s32[4]{0:T(128)} %param.23) | copy-start | bytes 52
  80.0 21.2 %copy-start.19 = (bf16[384,48]{0,1:T(8,128)(2,1)S(1)}, bf16[384,48]{0,1:T(8,128)(2,1)}, u32[]{:S(2)}) copy-start(bf16[384,48]{0,1:T(8,128)(2,1)} %param.28) | copy-start | bytes 110596
  80.0 43.4 %copy-start.17 = (f32[4,128]{1,0:T(4,128)}, f32[4,128]{1,0:T(4,128)S(1)}, u32[]{:S(2)}) copy-start(f32[4,128]{1,0:T(4,128)S(1)} %broadcast_multiply_fusion.1) | copy-start | bytes 6148
  81.6 2.1 copy-start.22
  81.6 2.1 copy-start.20
  82.9 67.4 %all-gather.11.cloned.1.call-start = ((), (), s32[]{:S(2)}) async-start(), calls=%async_computation.9 | async-start | bytes 1880064 | tf_op jit(solution)/shard_map/all_gather | solution.py:79
  83.6 115.7 %reduce-scatter.10.cloned.1.call-start = ((), (), s32[]{:S(2)}) async-start(), calls=%async_computation.10 | async-start | bytes 2359296 | tf_op jit(solution)/shard_map/reduce_scatter | solution.py:102
  170.4 3.8 copy-start.7
  174.2 69.9 %all-gather.15.cloned.1.call-start = ((), (), s32[]{:S(2)}) async-start(), calls=%async_computation.12 | async-start | bytes 2506752 | tf_op jit(solution)/shard_map/all_gather | solution.py:90
  174.8 97.4 %all-gather.13.cloned.1.call-start = ((), (), s32[]{:S(2)}) async-start(), calls=%async_computation.11 | async-start | bytes 2359296 | tf_op jit(solution)/shard_map/all_gather | solution.py:98
  202.7 98.7 %all-gather.19.cloned.1.call-start = ((), (), s32[]{:S(2)}) async-start(), calls=%async_computation.15 | async-start | bytes 2359296 | tf_op jit(solution)/shard_map/all_gather | solution.py:108
  205.7 140.6 %all-gather.17.cloned.1.call-start = ((), (), s32[]{:S(2)}) async-start(), calls=%async_computation.13 | async-start | bytes 2506752 | tf_op jit(solution)/shard_map/all_gather | solution.py:92
  206.5 180.6 %reduce-scatter.14.cloned.1.call-start = ((), (), s32[]{:S(2)}) async-start(), calls=%async_computation.16 | async-start | bytes 2359296 | tf_op jit(solution)/shard_map/reduce_scatter | solution.py:112
  278.3 2.7 copy-start.9
  346.3 12.0 %copy-start.27 = (bf16[768,1536]{1,0:T(8,128)(2,1)S(1)}, bf16[768,1536]{1,0:T(8,128)(2,1)}, u32[]{:S(2)}) copy-start(bf16[768,1536]{1,0:T(8,128)(2,1)} %all-gather.15.cloned.1.call-done) | copy-start | bytes 7077892
  362.1 57.0 %all-gather.21.cloned.1.call-start = ((), (), s32[]{:S(2)}) async-start(), calls=%async_computation.17 | async-start | bytes 2359296 | tf_op jit(solution)/shard_map/all_gather | solution.py:108
  391.8 96.1 %reduce-scatter.16.cloned.1.call-start = ((), (), s32[]{:S(2)}) async-start(), calls=%async_computation.18 | async-start | bytes 2359296 | tf_op jit(solution)/shard_map/reduce_scatter | solution.py:112
  453.4 112.0 %reduce-scatter.12.cloned.1.call-start = ((), (), s32[]{:S(2)}) async-start(), calls=%async_computation.14 | async-start | bytes 2359296 | tf_op jit(solution)/shard_map/reduce_scatter | solution.py:102
  459.9 110.9 %reduce-scatter.20.cloned.1.call-start = ((), (), s32[]{:S(2)}) async-start(), calls=%async_computation.20 | async-start | bytes 1253376 | tf_op jit(solution)/shard_map/reduce_scatter | solution.py:290
  463.6 186.1 %reduce-scatter.22.cloned.1.call-start = ((), (), s32[]{:S(2)}) async-start(), calls=%async_computation.21 | async-start | bytes 5013504 | tf_op jit(solution)/shard_map/reduce_scatter | solution.py:241
  470.8 258.3 %reduce-scatter.24.cloned.1.call-start = ((), (), s32[]{:S(2)}) async-start(), calls=%async_computation.22 | async-start | bytes 5013504 | tf_op jit(solution)/shard_map/reduce_scatter | solution.py:243
  478.3 322.2 %reduce-scatter.18.cloned.1.call-start = ((), (), s32[]{:S(2)}) async-start(), calls=%async_computation.19 | async-start | bytes 3760128 | tf_op jit(solution)/shard_map/reduce_scatter | solution.py:288
  484.1 2.0 copy-start.24
  487.5 2.4 copy-start.23
  487.5 2.4 copy-start.4
  487.5 2.4 copy-start.6
  487.6 2.4 copy-start.21
  487.9 2.1 copy-start.8
  (16 other events, 21.9 us)
Sparse Core Ops, SparseCore 0:
  83.0 24.4 all-gather.8
  109.8 40.3 all-gather.10
  174.3 24.9 reduce-scatter.9
  201.7 42.3 all-gather.14
  246.1 25.9 all-gather.12
  274.2 27.2 all-gather.18
  304.0 42.3 all-gather.16
  362.2 24.8 reduce-scatter.13
  391.9 27.2 all-gather.20
  453.5 26.0 reduce-scatter.15
  481.9 26.5 reduce-scatter.11
  512.6 58.1 reduce-scatter.19
  575.2 74.5 reduce-scatter.21
  654.5 74.5 reduce-scatter.23
  733.4 67.0 reduce-scatter.17
where the time goes:
time: 817 us; the launch traced here: 808 us
  waiting for transfers between devices  452 us (55%)
  blocking collectives  170 us (21%)
  matrix products  82.4 us (10%)
  other arithmetic  44.4 us (5%)
  local copies, waits for them, and re-layouts  38 us (5%)
  between operations  18.8 us (2%)
    unnamed x2, blocking collectives  123 us
    reduce_scatter x1, waiting for transfers between devices, on_device(): lax.psum_scatter(grad_downward, 'fsdp', scatter_dimension=1, tiled=True)  79.4 us
    reduce_scatter x1, waiting for transfers between devices, on_device(): lax.psum_scatter(grad_upward, 'fsdp', scatter_dimension=0, tiled=True)  79 us
    reduce_scatter x1, waiting for transfers between devices, on_device(): lax.psum_scatter(grad_joint_weight, 'fsdp', scatter_dimension=0, tiled=True)  71.4 us
    all_gather x1, waiting for transfers between devices, gather_dense(): lax.all_gather(pieces[4], 'fsdp', axis=1, tiled=True)  44.9 us
    all_gather x1, waiting for transfers between devices, gather_dense(): lax.all_gather(pieces[2], 'fsdp', axis=0, tiled=True)  37.4 us
    all_gather x2, waiting for transfers between devices, spread_grads(): return lax.all_gather(values, 'tp', axis=1, tiled=True)  32 us
    all_gather x2, waiting for transfers between devices, spread_rows(): return lax.all_gather(values, 'tp', axis=1, tiled=True)  28.1 us
  transfers between devices with their start and end apart: 15, of which 12 were waited for; matrix products, arithmetic and copies ran while one was open for 9% of the time, Pallas kernels for 0%

commit v1 on v0

v1 whole, which is shorter than its diff:
```python
from functools import partial

import jax
import jax.numpy as jnp
from jax import lax
from jax.sharding import PartitionSpec as P

HD = 64
SEQ = 197
SMALL = 128

norm_epsilon = 1e-06
masked_score = -1e30
f32 = jnp.float32
bf16 = jnp.bfloat16


def normalize(values, norm_gain, norm_shift):
    centre = values - jnp.mean(values, axis=-1, keepdims=True)
    spread = jnp.mean(centre * centre, axis=-1, keepdims=True)
    return centre * lax.rsqrt(spread + norm_epsilon) * norm_gain + norm_shift


def normalize_back(values, norm_gain, grad):
    centre = values - jnp.mean(values, axis=-1, keepdims=True)
    spread = jnp.mean(centre * centre, axis=-1, keepdims=True)
    rate = lax.rsqrt(spread + norm_epsilon)
    normal = centre * rate
    scaled = grad * norm_gain
    grad_values = rate * (
        scaled
        - jnp.mean(scaled, axis=-1, keepdims=True)
        - normal * jnp.mean(scaled * normal, axis=-1, keepdims=True)
    )
    return grad_values, jnp.sum(grad * normal, axis=0), jnp.sum(grad, axis=0)


class Exchange:
    def __init__(self, fsdp, tp):
        self.fsdp = fsdp
        self.tp = tp
        self.bits = fsdp.bit_length() - 1
        self.f = lax.axis_index("fsdp")
        self.y = lax.axis_index("tp")

    def side(self, bit):
        return self.y if bit == "y" else (self.f >> bit) & 1

    def swap(self, value, bit):
        if bit == "y":
            return lax.ppermute(value, "tp", [(0, 1), (1, 0)])
        return lax.ppermute(value, "fsdp", [(i, i ^ (1 << bit)) for i in range(self.fsdp)])

    def axis(self, bit):
        return self.bits + 1 if bit == "y" else self.bits - 1 - bit

    def spread_once(self, value, bit):
        other = self.swap(value, bit)
        first = self.side(bit) == 0
        return jnp.concatenate(
            [jnp.where(first, value, other), jnp.where(first, other, value)], axis=self.axis(bit)
        )

    def fold_once(self, value, bit):
        axis = self.axis(bit)
        size = value.shape[axis] // 2
        side = self.side(bit)
        sent = lax.dynamic_slice_in_dim(value, (1 - side) * size, size, axis)
        kept = lax.dynamic_slice_in_dim(value, side * size, size, axis)
        return kept + self.swap(sent, bit)

    def far_bits(self):
        return list(range(2, self.bits))

    def spread(self, value, order):
        for bit in order:
            value = self.spread_once(value, bit)
        return value

    def fold(self, value, order):
        for bit in order:
            value = self.fold_once(value, bit)
        return value

    def opened(self, shard):
        return shard.reshape((1,) * self.bits + shard.shape)

    def whole(self, gathered):
        return gathered.reshape(-1, gathered.shape[-1])

    def cut(self, whole):
        rows, columns = whole.shape
        return whole.reshape((2,) * self.bits + (rows // self.fsdp, columns))


def head_rows(flat):
    images, length, columns = flat.shape
    return flat.reshape(images, length, columns // HD, HD)


def on_device(
    fsdp,
    tp,
    tokens,
    cotangent,
    image_counts,
    split_points,
    attend_gain,
    attend_shift,
    qkv_weight,
    query_value_bias,
    output_weight,
    output_bias,
    dense_gain,
    dense_shift,
    up_weight,
    up_bias,
    down_weight,
    down_bias,
):
    ex = Exchange(fsdp, tp)
    y = ex.y
    slots, slot_count, width = tokens.shape
    images = slots // 2
    rows = width // fsdp
    half = output_weight.shape[0]
    hidden_half = up_weight.shape[1]
    scaling = HD ** (-0.5)
    far = ex.far_bits()

    own_start = y * images
    other_start = (1 - y) * images

    def take(array, start):
        return lax.dynamic_slice_in_dim(array, start, images, 0)

    def rows_of(array):
        other = ex.swap(take(array, other_start), "y")
        return jnp.concatenate([take(array, own_start), other], axis=1)

    def rows_back(array, kind):
        own, other = array[:, :slot_count], array[:, slot_count:].astype(bf16)
        back = ex.swap(other, "y").astype(kind)
        own = own.astype(kind)
        first = y == 0
        return jnp.concatenate([jnp.where(first, own, back), jnp.where(first, back, own)], axis=0)

    place = jnp.arange(slot_count)
    points = take(split_points, own_start)
    own_bound = jnp.where(y == 0, points, SEQ - points)
    bounds = jnp.stack([own_bound, SEQ - own_bound], axis=1)
    keys_live = (place[None, None, :] < bounds[:, :, None]).reshape(images, 2 * slot_count)
    live_images = own_start + jnp.arange(images) < image_counts[0]
    row_live = (live_images[:, None] & keys_live).astype(f32)[:, :, None]

    small = jnp.concatenate(
        [
            attend_gain,
            attend_shift,
            output_bias,
            dense_gain,
            dense_shift,
            down_bias,
            query_value_bias.reshape(-1),
            up_bias,
        ]
    )
    small_size = small.shape[0]
    small = jnp.pad(small, (0, rows * SMALL - small_size)).reshape(rows, SMALL)
    attend_shard = jnp.concatenate(
        [qkv_weight.reshape(rows, 3 * half), output_weight.T, small], axis=1
    )
    cut_at = 2 * half
    token_rows = rows_of(tokens)
    attend_far = ex.spread(ex.opened(attend_shard), far)
    attend_one = ex.spread(attend_far[..., :cut_at], [1, "y", 0])
    attend_two = ex.spread(attend_far[..., cut_at:], ["y", 1, 0])
    up_whole = ex.whole(ex.spread(ex.opened(up_weight), far + [1, "y", 0]))
    down_whole = ex.whole(ex.spread(ex.opened(down_weight.T), far + ["y", 1, 0]))
    grad_rows = rows_of(cotangent)

    one = ex.whole(attend_one).reshape(width, 2, 2, half)
    two = ex.whole(attend_two).reshape(width, 2, 2 * half + SMALL)
    query_matrix = one[:, :, 0].reshape(width, 2 * half)
    key_matrix = one[:, :, 1].reshape(width, 2 * half)
    value_matrix = two[:, :, :half].reshape(width, 2 * half)
    output_turned = two[:, :, half : 2 * half].reshape(width, 2 * half)
    joint_matrix = jnp.concatenate([query_matrix, key_matrix, value_matrix], axis=1)
    small_all = two[:, :, 2 * half :].reshape(fsdp, rows, 2, SMALL).transpose(2, 0, 1, 3)
    small_all = small_all.reshape(2, fsdp, rows * SMALL)[:, :, :small_size].astype(f32)
    plain = small_all[0, :, : 6 * rows].reshape(fsdp, 6, rows).transpose(1, 0, 2).reshape(6, width)
    first_gain, first_shift, output_add, second_gain, second_shift, down_add = (
        plain[i] for i in range(6)
    )
    short = rows // 2
    joint_add = small_all[:, :, 6 * rows : 7 * rows].reshape(2, fsdp, 2, short)
    joint_add = joint_add.transpose(2, 0, 1, 3).reshape(2, width)
    up_add = small_all[:, :, 7 * rows :].reshape(-1)

    length = 2 * slot_count
    inputs = token_rows.astype(f32)
    first_rows = normalize(inputs, first_gain, first_shift).astype(bf16)
    joint = jnp.einsum("gsd,dn->gsn", first_rows, joint_matrix, preferred_element_type=f32)
    query_rows = head_rows((joint[..., :width] + joint_add[0]).astype(bf16))
    key_rows = head_rows(joint[..., width : 2 * width].astype(bf16))
    value_rows = head_rows((joint[..., 2 * width :] + joint_add[1]).astype(bf16))
    scores = jnp.einsum("bqhe,bkhe->bhqk", query_rows, key_rows, preferred_element_type=f32)
    scores = jnp.where(keys_live[:, None, None, :], scores * scaling, masked_score)
    row_top = jnp.max(scores, axis=-1, keepdims=True)
    raised = jnp.exp(scores - row_top)
    row_total = jnp.sum(raised, axis=-1, keepdims=True)
    chances = raised / row_total
    rounded = chances.astype(bf16)
    mixed = jnp.einsum("bhqk,bkhe->bqhe", rounded, value_rows, preferred_element_type=f32)
    mixed = mixed.astype(bf16).reshape(images, length, width)
    branch = jnp.einsum("gsn,dn->gsd", mixed, output_turned, preferred_element_type=f32)
    middle = inputs + branch + output_add

    second_rows = normalize(middle, second_gain, second_shift).astype(bf16)
    hidden = jnp.einsum("gsd,df->gsf", second_rows, up_whole, preferred_element_type=f32) + up_add
    active, gelu_back = jax.vjp(partial(jax.nn.gelu, approximate=False), hidden)
    active = active.astype(bf16)
    grad_out = grad_rows.astype(f32) * row_live
    grad_down_in = grad_out.astype(bf16)
    grad_down = jnp.einsum("gsd,gsf->df", grad_down_in, active, preferred_element_type=f32)
    grad_down = ex.fold(ex.cut(grad_down.astype(bf16)), [0, "y", 1] + far[::-1])
    dense_out = jnp.einsum("gsf,df->gsd", active, down_whole, preferred_element_type=f32)
    result = (middle + dense_out + down_add) * row_live
    out_tokens = rows_back(result.astype(bf16), bf16)
    grad_active = jnp.einsum("gsd,df->gsf", grad_down_in, down_whole, preferred_element_type=f32)
    grad_hidden = gelu_back(grad_active)[0].astype(bf16)
    grad_up = jnp.einsum("gsd,gsf->df", second_rows, grad_hidden, preferred_element_type=f32)
    grad_up = ex.fold(ex.cut(grad_up.astype(bf16)), [0, 1, "y"] + far[::-1])
    grad_up_add = jnp.sum(grad_hidden, axis=(0, 1), dtype=f32)
    grad_second = jnp.einsum("gsf,df->gsd", grad_hidden, up_whole, preferred_element_type=f32)
    flat = (images * length, width)
    grad_middle_norm, grad_second_gain, grad_second_shift = normalize_back(
        middle.reshape(flat), second_gain, grad_second.reshape(flat)
    )
    grad_middle = grad_out + grad_middle_norm.reshape(images, length, width)
    grad_down_add = jnp.sum(grad_out, axis=(0, 1))
    grad_output_add = jnp.sum(grad_middle, axis=(0, 1))

    grad_branch = grad_middle.astype(bf16)
    grad_output = jnp.einsum("gsd,gsn->dn", grad_branch, mixed, preferred_element_type=f32)
    grad_mixed = jnp.einsum("gsd,dn->gsn", grad_branch, output_turned, preferred_element_type=f32)
    grad_mixed = head_rows(grad_mixed.astype(bf16))
    grad_value = jnp.einsum("bhqk,bqhe->bkhe", rounded, grad_mixed, preferred_element_type=f32)
    grad_chance = jnp.einsum("bqhe,bkhe->bhqk", grad_mixed, value_rows, preferred_element_type=f32)
    centred = grad_chance - jnp.sum(chances * grad_chance, axis=-1, keepdims=True)
    grad_scores = (chances * centred).astype(bf16)
    grad_query = jnp.einsum("bhqk,bkhe->bqhe", grad_scores, key_rows, preferred_element_type=f32)
    grad_key = jnp.einsum("bhqk,bqhe->bkhe", grad_scores, query_rows, preferred_element_type=f32)
    grad_joint = jnp.concatenate(
        [
            (part * scale).astype(bf16).reshape(images, length, width)
            for part, scale in ((grad_query, scaling), (grad_key, scaling), (grad_value, 1.0))
        ],
        axis=-1,
    )
    grad_joint_matrix = jnp.einsum("gsd,gsn->dn", first_rows, grad_joint, preferred_element_type=f32)
    grad_joint_add = jnp.sum(grad_joint, axis=(0, 1), dtype=f32).reshape(3, width)
    grad_first = jnp.einsum("gsn,dn->gsd", grad_joint, joint_matrix, preferred_element_type=f32)
    grad_inputs_norm, grad_first_gain, grad_first_shift = normalize_back(
        inputs.reshape(flat), first_gain, grad_first.reshape(flat)
    )
    grad_tokens = rows_back(grad_middle + grad_inputs_norm.reshape(images, length, width), f32)

    plain_grads = jnp.stack(
        [
            grad_first_gain,
            grad_first_shift,
            grad_output_add,
            grad_second_gain,
            grad_second_shift,
            grad_down_add,
        ]
    )
    plain_grads = plain_grads.reshape(6, fsdp, rows).transpose(1, 0, 2).reshape(1, fsdp, 6 * rows)
    plain_grads = jnp.broadcast_to(plain_grads, (2, fsdp, 6 * rows))
    bias_grads = grad_joint_add[0::2].reshape(2, 2, fsdp, short).transpose(1, 2, 0, 3)
    bias_grads = bias_grads.reshape(2, fsdp, rows)
    up_grads = grad_up_add.reshape(2, fsdp, 2 * rows)
    small_grads = jnp.concatenate([plain_grads, bias_grads, up_grads], axis=-1)
    small_grads = jnp.pad(small_grads, ((0, 0), (0, 0), (0, rows * SMALL - small_size)))
    small_grads = small_grads.reshape(2, width, SMALL).transpose(1, 0, 2).astype(bf16)
    joint_parts = grad_joint_matrix.astype(bf16).reshape(width, 3, 2, half)
    part_one = jnp.concatenate([joint_parts[:, 0], joint_parts[:, 1]], axis=-1)
    part_two = jnp.concatenate(
        [joint_parts[:, 2], grad_output.astype(bf16).reshape(width, 2, half), small_grads], axis=-1
    )
    part_one = ex.fold(ex.cut(part_one.reshape(width, -1)), [0, "y", 1])
    part_two = ex.fold(ex.cut(part_two.reshape(width, -1)), [0, 1, "y"])
    attend_grads = ex.fold(jnp.concatenate([part_one, part_two], axis=-1), far[::-1])
    attend_grads = ex.whole(attend_grads)
    grad_qkv = attend_grads[:, : 3 * half].astype(f32).reshape(rows, 3, half)
    grad_output = attend_grads[:, 3 * half : 4 * half].astype(f32).T
    small_home = attend_grads[:, 4 * half :].reshape(-1)[:small_size].astype(f32)
    plain_home = small_home[: 6 * rows].reshape(6, rows)
    return (
        out_tokens,
        grad_tokens,
        plain_home[0],
        plain_home[1],
        grad_qkv,
        small_home[6 * rows : 7 * rows].reshape(2, short),
        grad_output,
        plain_home[2],
        plain_home[3],
        plain_home[4],
        ex.whole(grad_up).astype(f32),
        small_home[7 * rows :],
        ex.whole(grad_down).astype(f32).T,
        plain_home[5],
    )


def solution(mesh):
    return jax.shard_map(
        partial(on_device, mesh.shape["fsdp"], mesh.shape["tp"]),
        mesh=mesh,
        in_specs=(
            P("fsdp", "tp", None),
            P("fsdp", "tp", None),
            P("fsdp"),
            P("fsdp"),
            P("fsdp"),
            P("fsdp"),
            P("fsdp", None, "tp"),
            P(None, ("tp", "fsdp")),
            P("tp", "fsdp"),
            P("fsdp"),
            P("fsdp"),
            P("fsdp"),
            P("fsdp", "tp"),
            P(("tp", "fsdp")),
            P("tp", "fsdp"),
            P("fsdp"),
        ),
        out_specs=(
            P("fsdp", "tp", None),
            P("fsdp", "tp", None),
            P("fsdp"),
            P("fsdp"),
            P("fsdp", None, "tp"),
            P(None, ("tp", "fsdp")),
            P("tp", "fsdp"),
            P("fsdp"),
            P("fsdp"),
            P("fsdp"),
            P("fsdp", "tp"),
            P(("tp", "fsdp")),
            P("tp", "fsdp"),
            P("fsdp"),
        ),
        check_vma=False,
    )
```

time: 817 us -> 491 us (0.60)
  waiting for transfers between devices: 452 us -> 170 us
  blocking collectives: 170 us -> 0 us
  local copies, waits for them, and re-layouts: 38 us -> 114 us
  starting transfers between devices: 1.25 us -> 40.5 us
  other arithmetic: 44.4 us -> 75.5 us
  between operations: 18.8 us -> 3.12 us
    reduce_scatter x8 -> x0, waiting for transfers between devices: 281 us -> none  [the longest x1 79.4 us: on_device(): lax.psum_scatter(grad_downward, 'fsdp', scatter_dimension=1, tiled=True)]
    ppermute x0 -> x40, waiting for transfers between devices: none -> 170 us  [the longest x28 134 us: swap(): lax.ppermute(value, 'fsdp', [(i, i ^ 1 << bit) for i in range(self.fsdp)])]
    all_gather x7 -> x0, waiting for transfers between devices: 169 us -> none  [the longest x1 44.9 us: gather_dense(): lax.all_gather(pieces[4], 'fsdp', axis=1, tiled=True)]
    unnamed x2 -> x0, blocking collectives: 123 us -> none
    ppermute x0 -> x40, starting transfers between devices: none -> 40.5 us  [the longest x28 27.3 us: swap(): lax.ppermute(value, 'fsdp', [(i, i ^ 1 << bit) for i in range(self.fsdp)])]
    all_gather x2 -> x0, blocking collectives: 39.2 us -> none  [the longest x1 22.2 us: gather_attend(): lax.all_gather(pieces[4], 'fsdp', axis=1, tiled=True)]
    another operation x13 -> x16, local copies, waits for them, and re-layouts: 9.16 us -> 31.8 us  [the longest x2 11.6 us: cut(): return whole.reshape((2,) * self.bits + (rows // self.fsdp, columns))]
    reshape x0 -> x16, local copies, waits for them, and re-layouts: none -> 21.5 us  [the longest x1 6.47 us: on_device(): joint_parts = grad_joint_matrix.astype(bf16).reshape(width, 3, 2, half)]
  transfers between devices with their start and end apart: 15 -> 40, of which waited for: 12 -> 22; matrix products, arithmetic and copies ran while one was open for 9% -> 42% of each run, Pallas kernels for 0% -> 0%
where the time goes in v1:
time: 491 us; the launch traced here: 484 us
  waiting for transfers between devices  170 us (35%)
  local copies, waits for them, and re-layouts  114 us (23%)
  matrix products  80.7 us (16%)
  other arithmetic  75.5 us (15%)
  starting transfers between devices  40.5 us (8%)
    ppermute x28, waiting for transfers between devices, swap(): lax.ppermute(value, 'fsdp', [(i, i ^ 1 << bit) for i in range(self.fsdp)])  134 us
    ppermute x12, waiting for transfers between devices, swap(): return lax.ppermute(value, 'tp', [(0, 1), (1, 0)])  35.4 us
    ppermute x28, starting transfers between devices, swap(): lax.ppermute(value, 'fsdp', [(i, i ^ 1 << bit) for i in range(self.fsdp)])  27.3 us
    convert_element_type x1, other arithmetic, on_device(): active = active.astype(bf16)  15.4 us
    ppermute x12, starting transfers between devices, swap(): return lax.ppermute(value, 'tp', [(0, 1), (1, 0)])  13.2 us
    slice x2, local copies, waits for them, and re-layouts, on_device(): query_matrix = one[:, :, 0].reshape(width, 2 * half)  12 us
    another operation x2, local copies, waits for them, and re-layouts, cut(): return whole.reshape((2,) * self.bits + (rows // self.fsdp, columns))  11.6 us
    concatenate x19, other arithmetic, spread_once(): jnp.concatenate([jnp.where(first, value, other), jnp.where(first, other,...  9.99 us
  transfers between devices with their start and end apart: 40, of which 22 were waited for; matrix products, arithmetic and copies ran while one was open for 42% of the time, Pallas kernels for 0%

profile of v1, /device:TPU:0, one launch (start us, length us, event | category | flops | bytes accessed | tf_op | source)
XLA Modules:
  0.0 483.7 jit_solution(4851087020822050344)
XLA Ops:
  27.5 19.2 %collective-permute-done.15 = bf16[1,2,1,1,48,1536]{5,4,3,2,1,0:T(8,128)(2,1)S(1)} collective-permute-done((bf16[1,2,1,1,48,1536]{5,4,3,2,1,0:T(8,128)(2,1)S(1)}, bf16[1,2,1,1,48,1536]{5,4,3,2,1,0:T(8,128)(2,1)S(1)}, u32[]{:S(2)}, u32[]{:S(2)}) %collective-permute-start.15) | collective-permute-done | bytes 294944 | tf_op jit(solution)/shard_map/ppermute | solution.py:52
  53.1 6.7 %collective-permute-done.2 = bf16[1,2,1,1,48,1664]{5,4,3,2,1,0:T(8,128)(2,1)S(1)} collective-permute-done((bf16[1,2,1,1,48,1664]{5,4,3,2,1,0:T(8,128)(2,1)S(1)}, bf16[1,2,1,1,48,1664]{5,4,3,2,1,0:T(8,128)(2,1)S(1)}, u32[]{:S(2)}, u32[]{:S(2)}) %collective-permute-start.2) | collective-permute-done | bytes 319520 | tf_op jit(solution)/shard_map/ppermute | solution.py:52
  63.8 6.0 %collective-permute-done.6 = bf16[2,2,1,1,48,768]{5,4,3,2,1,0:T(8,128)(2,1)S(1)} collective-permute-done((bf16[2,2,1,1,48,768]{5,4,3,2,1,0:T(8,128)(2,1)S(1)}, bf16[2,2,1,1,48,768]{5,4,3,2,1,0:T(8,128)(2,1)S(1)}, u32[]{:S(2)}, u32[]{:S(2)}) %collective-permute-start.6) | collective-permute-done | bytes 294944 | tf_op jit(solution)/shard_map/ppermute | solution.py:52
  74.9 7.6 %collective-permute-done.11 = bf16[2,2,1,1,48,1536]{5,4,3,2,1,0:T(8,128)(2,1)S(1)} collective-permute-done((bf16[2,2,1,1,48,1536]{5,4,3,2,1,0:T(8,128)(2,1)S(1)}, bf16[2,2,1,1,48,1536]{5,4,3,2,1,0:T(8,128)(2,1)S(1)}, u32[]{:S(2)}, u32[]{:S(2)}) %collective-permute-start.11) | collective-permute-done | bytes 589856 | tf_op jit(solution)/shard_map/ppermute | solution.py:52
  85.2 12.0 %collective-permute-done.4 = bf16[2,2,1,1,48,1792]{5,4,3,2,1,0:T(8,128)(2,1)S(1)} collective-permute-done((bf16[2,2,1,1,48,1792]{5,4,3,2,1,0:T(8,128)(2,1)S(1)}, bf16[2,2,1,1,48,1792]{5,4,3,2,1,0:T(8,128)(2,1)S(1)}, u32[]{:S(2)}, u32[]{:S(2)}) %collective-permute-start.4) | collective-permute-done | bytes 688160 | tf_op jit(solution)/shard_map/ppermute | solution.py:52
  99.0 22.6 %collective-permute-done.17 = bf16[2,2,1,1,48,3072]{5,4,3,2,1,0:T(8,128)(2,1)S(1)} collective-permute-done((bf16[2,2,1,1,48,3072]{5,4,3,2,1,0:T(8,128)(2,1)S(1)}, bf16[2,2,1,1,48,3072]{5,4,3,2,1,0:T(8,128)(2,1)S(1)}, u32[]{:S(2)}, u32[]{:S(2)}) %collective-permute-start.17) | collective-permute-done | bytes 1179680 | tf_op jit(solution)/shard_map/ppermute | solution.py:52
  129.1 5.1 %reshape_reshape.13 = bf16[768,2,2,384]{3,2,1,0:T(2,128)(2,1)S(1)} reshape(bf16[2,2,2,2,48,1536]{5,4,3,2,1,0:T(8,128)(2,1)} %pad_maximum_fusion.4) | data formatting | bytes 4718592 | tf_op jit(solution)/shard_map/reshape;reshape | solution.py:182
  134.2 5.4 %fusion.69 = (bf16[768,2,1,384]{3,2,1,0:T(2,128)(2,1)}, bf16[768,2,1,384]{3,2,1,0:T(2,128)(2,1)}) fusion(bf16[768,2,2,384]{3,2,1,0:T(2,128)(2,1)S(1)} %reshape_reshape.13), kind=kLoop, calls=%fused_computation.256 | loop fusion | bytes 4718592 | tf_op jit(solution)/shard_map/slice | solution.py:184
  139.6 6.6 %copy.76 = bf16[768,2,1,384]{0,3,1,2:T(8,128)(2,1)} copy(bf16[768,2,1,384]{3,2,1,0:T(2,128)(2,1)} %get-tuple-element.85) | data formatting | bytes 2359296 | tf_op jit(solution)/shard_map/slice | solution.py:184
  148.6 4.9 %copy.77 = bf16[768,2,1,384]{0,3,1,2:T(8,128)(2,1)} copy(bf16[768,2,1,384]{3,2,1,0:T(2,128)(2,1)S(1)} %copy-done.12) | data formatting | bytes 2359296 | tf_op jit(solution)/shard_map/slice | solution.py:185
  159.3 5.3 %reshape_reshape.12 = bf16[768,2,896]{2,1,0:T(2,128)(2,1)S(1)} reshape(bf16[2,2,2,2,48,1792]{5,4,3,2,1,0:T(8,128)(2,1)} %pad_maximum_fusion.2) | data formatting | bytes 5505024 | tf_op jit(solution)/shard_map/reshape;reshape | solution.py:183
  186.7 6.3 %fusion.72 = (f32[2,12,256]{2,1,0:T(8,128)}, f32[2,12,256,256]{2,3,1,0:T(8,128)}) fusion(pred[2,256]{1,0:T(4,128)(4,1)} %get-tuple-element.63, bf16[2,256,12,64]{1,3,2,0:T(8,128)(2,1)S(1)} %bitcast.188, bf16[2,256,12,64]{1,3,2,0:T(8,128)(2,1)S(1)} %bitcast.190), kind=kOutput, calls=%fused_computation.259 | convolution fusion | flops 207618304 | bytes 7889408 | tf_op jit(solution)/shard_map/sub | solution.py:210
  206.6 15.4 %multiply_convert_fusion.1 = (bf16[2,256,3072]{2,1,0:T(8,128)(2,1)}, f32[2,256,3072]{2,1,0:T(8,128)S(1)}) fusion(f32[2,256,3072]{2,1,0:T(8,128)S(1)} %get-tuple-element.139, f32[3072]{0:T(1024)S(1)} %add.281, u8[256,3072]{1,0:T(8,128)(4,1)S(1)} %get-tuple-element.43, u8[256,3072]{1,0:T(8,128)(4,1)S(1)} %get-tuple-element.42), kind=kLoop, calls=%fused_computation.14 | loop fusion | flops 111673344 | bytes 17313792 | tf_op jit(solution)/shard_map/convert_element_type | solution.py:222
  224.6 8.1 %fusion.74 = (bf16[3072]{0:T(1024)(128)(2,1)}, bf16[2,256,3072]{2,1,0:T(8,128)(2,1)}) fusion(f32[2,256,3072]{2,1,0:T(8,128)S(1)} %get-tuple-element.65, bf16[768,3072,1]{1,0,2:T(8,128)(2,1)S(1)} %bitcast.183, f32[2,256]{1,0:T(2,128)S(1)} %copy-done.56, bf16[2,128,768]{2,1,0:T(8,128)(2,1)} %collective-permute-done.20, ...), kind=kOutput, calls=%fused_computation.261 | convolution fusion | flops 2443441152 | bytes 21254144 | tf_op jit(solution)/shard_map/gsd,df->gsf/dot_general | solution.py:230
  232.7 6.7 %bitcast_convert_fusion.1 = bf16[768,3072]{1,0:T(8,128)(2,1)} fusion(bf16[2,256,3072]{2,1,0:T(8,128)(2,1)} %get-tuple-element.141, f32[2,256,768]{2,1,0:T(8,128)S(1)} %get-tuple-element.138, f32[768]{0:T(1024)S(1)} %copy-done.67, f32[768]{0:T(1024)S(1)} %copy-done.53, f32[2,256]{1,0:T(2,128)S(1)} %get-tuple-element.132, f32[2,256]{1,0:T(2,128)S(1)} %get-tuple-element.134), kind=kOutput, calls=%fused_computation.3 | convolution fusion | flops 2420244480 | bytes 9447424 | tf_op jit(solution)/shard_map/gsd,gsf->df/dot_general | solution.py:232
  239.5 6.0 %multiply_reduce_fusion.1 = (bf16[768]{0:T(1024)(128)(2,1)}, f32[512]{0:T(512)S(1)}, f32[512]{0:T(512)S(1)}, bf16[768]{0:T(1024)(128)(2,1)}, f32[512,768]{1,0:T(8,128)S(1)}) fusion(f32[2,256,768]{2,1,0:T(8,128)S(1)} %get-tuple-element.138, f32[512]{0:T(512)S(1)} %bitcast.219, f32[512]{0:T(512)S(1)} %bitcast.221, f32[768]{0:T(1024)S(1)} %copy-done.53, ...), kind=kOutput, calls=%fused_computation.81 | convolution fusion | flops 2419455488 | bytes 11024384 | tf_op jit(solution)/shard_map/gsf,df->gsd/dot_general | solution.py:235
  254.8 5.1 %fusion.41 = bf16[2,12,64,256]{3,2,1,0:T(8,128)(2,1)} fusion(bf16[2,256,12,64]{1,3,2,0:T(8,128)(2,1)} %bitcast.205, f32[2,12,256,256]{2,3,1,0:T(8,128)} %get-tuple-element.136, f32[2,12,256]{2,1,0:T(8,128)} %get-tuple-element.135), kind=kOutput, calls=%fused_computation.97 | convolution fusion | flops 204865536 | bytes 7888896 | tf_op jit(solution)/shard_map/bhqk,bqhe->bkhe/dot_general | solution.py:248
  259.9 6.8 %multiply_reduce_fusion = (f32[2,12,256]{2,1,0:T(8,128)S(1)}, f32[2,12,256,256]{2,3,1,0:T(8,128)}) fusion(f32[2,12,256,256]{2,3,1,0:T(8,128)} %get-tuple-element.136, f32[2,12,256]{2,1,0:T(8,128)S(1)} %copy-done.48, bf16[2,256,12,64]{1,3,2,0:T(8,128)(2,1)S(1)} %bitcast.206, bf16[2,256,12,64]{1,3,2,0:T(8,128)(2,1)S(1)} %bitcast.203), kind=kOutput, calls=%fused_computation.12 | convolution fusion | flops 206039040 | bytes 14204928 | tf_op jit(solution)/shard_map/bqhe,bkhe->bhqk/dot_general | solution.py:249
  276.1 6.4 %multiply_convert_fusion.4 = bf16[2,256,768]{2,1,0:T(8,128)(2,1)S(1)} fusion(f32[2,256,768]{2,1,0:T(8,128)} %copy-done.13, bf16[2,256,3072]{2,1,0:T(8,128)(2,1)} %get-tuple-element.64, bf16[768,3072,1]{1,0,2:T(8,128)(2,1)} %bitcast.184, f32[2,256]{1,0:T(2,128)S(1)} %copy-done.57, f32[768]{0:T(1024)S(1)} %copy-done.66), kind=kOutput, calls=%fused_computation.86 | convolution fusion | flops 2417491968 | bytes 10228736 | tf_op jit(solution)/shard_map/gsf,df->gsd/dot_general | solution.py:227
  301.6 5.0 %fusion.25 = (bf16[768]{0:T(1024)(128)(2,1)}, f32[2,256]{1,0:T(2,128)S(1)}, f32[2,256]{1,0:T(2,128)S(1)}, bf16[768]{0:T(1024)(128)(2,1)}, f32[2,256,768]{2,1,0:T(8,128)S(1)}) fusion(f32[2,256]{1,0:T(2,128)} %add_rsqrt_fusion.1, f32[2,256]{1,0:T(2,128)S(1)} %copy-done.50, bf16[2,128,768]{2,1,0:T(8,128)(2,1)S(1)} %copy-done.28, ...), kind=kOutput, calls=%fused_computation.68 | convolution fusion | flops 1834743296 | bytes 8271872 | tf_op jit(solution)/shard_map/gsn,dn->gsd/dot_general | solution.py:263
  315.5 5.4 %bitcast_convert_fusion.2 = bf16[768,2304]{1,0:T(8,128)(2,1)} fusion(f32[768]{0:T(1024)} %copy-done.65, f32[768]{0:T(1024)} %copy-done.51, f32[2,256]{1,0:T(2,128)} %add_rsqrt_fusion.1, f32[2,256]{1,0:T(2,128)} %copy-done.49, bf16[2,256,768]{2,1,0:T(8,128)(2,1)S(1)} %copy-done.33, bf16[2,256,768]{2,1,0:T(8,128)(2,1)} %copy.91, ...), kind=kOutput, calls=%fused_computation.4 | convolution fusion | flops 1824325632 | bytes 6694912 | tf_op jit(solution)/shard_map/gsd,gsn->dn/dot_general | solution.py:261
  320.9 6.5 %reshape.475 = bf16[768,3,2,384]{3,2,1,0:T(2,128)(2,1)S(1)} reshape(bf16[768,2304]{1,0:T(8,128)(2,1)} %bitcast_convert_fusion.2) | data formatting | bytes 7077888 | tf_op jit(solution)/shard_map/reshape | solution.py:287
  334.1 5.6 %reshape_reshape.14 = bf16[2,2,2,2,48,1536]{5,4,3,2,1,0:T(8,128)(2,1)S(1)} reshape(bf16[768,2,768]{2,1,0:T(2,128)(2,1)} %pad_maximum_fusion.8) | data formatting | bytes 4718592 | tf_op jit(solution)/shard_map/reshape;reshape | solution.py:93
  347.4 6.1 %reshape_reshape.15 = bf16[2,2,2,2,48,1792]{5,4,3,2,1,0:T(8,128)(2,1)S(1)} reshape(bf16[768,2,896]{2,1,0:T(2,128)(2,1)} %pad_maximum_fusion.3) | data formatting | bytes 5505024 | tf_op jit(solution)/shard_map/reshape;reshape | solution.py:93
  354.4 4.8 bitcast_convert_fusion
  368.4 8.8 %collective-permute-done.23 = bf16[2,2,2,1,48,768]{5,4,3,2,1,0:T(8,128)(2,1)S(1)} collective-permute-done((bf16[2,2,2,1,48,768]{5,4,3,2,1,0:T(8,128)(2,1)S(1)}, bf16[2,2,2,1,48,768]{5,4,3,2,1,0:T(8,128)(2,1)S(1)}, u32[]{:S(2)}, u32[]{:S(2)}) %collective-permute-start.23) | collective-permute-done | bytes 589856 | tf_op jit(solution)/shard_map/ppermute | solution.py:51
  382.1 5.1 %collective-permute-done.24 = bf16[2,2,1,1,48,768]{5,4,3,2,1,0:T(8,128)(2,1)S(1)} collective-permute-done((bf16[2,2,1,1,48,768]{5,4,3,2,1,0:T(8,128)(2,1)S(1)}, bf16[2,2,1,1,48,768]{5,4,3,2,1,0:T(8,128)(2,1)S(1)}, u32[]{:S(2)}, u32[]{:S(2)}) %collective-permute-start.24) | collective-permute-done | bytes 294944 | tf_op jit(solution)/shard_map/ppermute | solution.py:52
  391.3 14.6 %collective-permute-done.28 = bf16[1,2,1,1,48,1664]{5,4,3,2,1,0:T(8,128)(2,1)S(1)} collective-permute-done((bf16[1,2,1,1,48,1664]{5,4,3,2,1,0:T(8,128)(2,1)S(1)}, bf16[1,2,1,1,48,1664]{5,4,3,2,1,0:T(8,128)(2,1)S(1)}, u32[]{:S(2)}, u32[]{:S(2)}) %collective-permute-start.28) | collective-permute-done | bytes 319520 | tf_op jit(solution)/shard_map/ppermute | solution.py:52
  420.9 15.4 %collective-permute-done.36 = bf16[2,2,2,1,48,1536]{5,4,3,2,1,0:T(8,128)(2,1)} collective-permute-done((bf16[2,2,2,1,48,1536]{5,4,3,2,1,0:T(8,128)(2,1)}, bf16[2,2,2,1,48,1536]{5,4,3,2,1,0:T(8,128)(2,1)}, u32[]{:S(2)}, u32[]{:S(2)}) %collective-permute-start.36) | collective-permute-done | bytes 1179680 | tf_op jit(solution)/shard_map/ppermute | solution.py:51
  438.7 9.3 %collective-permute-done.32 = bf16[2,2,1,1,48,1536]{5,4,3,2,1,0:T(8,128)(2,1)S(1)} collective-permute-done((bf16[2,2,1,1,48,1536]{5,4,3,2,1,0:T(8,128)(2,1)S(1)}, bf16[2,2,1,1,48,1536]{5,4,3,2,1,0:T(8,128)(2,1)S(1)}, u32[]{:S(2)}, u32[]{:S(2)}) %collective-permute-start.32) | collective-permute-done | bytes 589856 | tf_op jit(solution)/shard_map/ppermute | solution.py:51
  454.0 16.8 %collective-permute-done.33 = bf16[1,2,1,1,48,1536]{5,4,3,2,1,0:T(8,128)(2,1)S(1)} collective-permute-done((bf16[1,2,1,1,48,1536]{5,4,3,2,1,0:T(8,128)(2,1)S(1)}, bf16[1,2,1,1,48,1536]{5,4,3,2,1,0:T(8,128)(2,1)S(1)}, u32[]{:S(2)}, u32[]{:S(2)}) %collective-permute-start.33) | collective-permute-done | bytes 294944 | tf_op jit(solution)/shard_map/ppermute | solution.py:52
  471.0 5.3 %collective-permute-done.38 = bf16[1,2,1,1,48,1536]{5,4,3,2,1,0:T(8,128)(2,1)S(1)} collective-permute-done((bf16[1,2,1,1,48,1536]{5,4,3,2,1,0:T(8,128)(2,1)S(1)}, bf16[1,2,1,1,48,1536]{5,4,3,2,1,0:T(8,128)(2,1)S(1)}, u32[]{:S(2)}, u32[]{:S(2)}) %collective-permute-start.38) | collective-permute-done | bytes 294944 | tf_op jit(solution)/shard_map/ppermute | solution.py:52
  (415 shorter events, 209.8 us)
Async XLA Ops:
  0.7 18.2 %collective-permute-start.14 = (bf16[1,1,1,1,48,1536]{5,4,3,2,1,0:T(8,128)(2,1)}, bf16[1,1,1,1,48,1536]{5,4,3,2,1,0:T(8,128)(2,1)S(1)}, u32[]{:S(2)}, u32[]{:S(2)}) collective-permute-start(bf16[1,1,1,1,48,1536]{5,4,3,2,1,0:T(8,128)(2,1)} %bitcast.213), channel_id=1, source_target_pairs={{0,8},{2,10},{4,12},{6,14},{8,0},{10,2},{12,4},{14,6},{16,24},{18,... | collective-permute-start | bytes 442376 | tf_op jit(solution)/shard_map/ppermute | solution.py:52
  3.8 17.9 %collective-permute-start.9 = (bf16[1,1,1,1,48,1536]{5,4,3,2,1,0:T(8,128)(2,1)}, bf16[1,1,1,1,48,1536]{5,4,3,2,1,0:T(8,128)(2,1)}, u32[]{:S(2)}, u32[]{:S(2)}) collective-permute-start(bf16[1,1,1,1,48,1536]{5,4,3,2,1,0:T(8,128)(2,1)} %bitcast.214), channel_id=1, source_target_pairs={{0,8},{2,10},{4,12},{6,14},{8,0},{10,2},{12,4},{14,6},{16,24},{18,... | collective-permute-start | bytes 442376 | tf_op jit(solution)/shard_map/ppermute | solution.py:52
  11.1 12.1 %collective-permute-start.1 = (bf16[1,1,1,1,48,1664]{5,4,3,2,1,0:T(8,128)(2,1)S(1)}, bf16[1,1,1,1,48,1664]{5,4,3,2,1,0:T(8,128)(2,1)S(1)}, u32[]{:S(2)}, u32[]{:S(2)}) collective-permute-start(bf16[1,1,1,1,48,1664]{5,4,3,2,1,0:T(8,128)(2,1)S(1)} %maximum_bitcast_fusion.3), channel_id=1, source_target_pairs={{0,8},{2,10},{4,12},{6,14},{8,0},{10,2},{12,4},{14,6},{16,24},{18,... | collective-permute-start | bytes 479240 | tf_op jit(solution)/shard_map/ppermute | solution.py:52
  14.2 12.1 %collective-permute-start = (bf16[2,128,768]{2,1,0:T(8,128)(2,1)S(1)}, bf16[2,128,768]{2,1,0:T(8,128)(2,1)S(1)}, u32[]{:S(2)}, u32[]{:S(2)}) collective-permute-start(bf16[2,128,768]{2,1,0:T(8,128)(2,1)S(1)} %get-tuple-element.106), channel_id=1, source_target_pairs={{0,1},{1,0},{2,3},{3,2},{4,5},{5,4},{6,7},{7,6},{8,9},{9,8},{10,11... | collective-permute-start | bytes 1179656 | tf_op jit(solution)/shard_map/ppermute | solution.py:51
  16.6 207.8 %collective-permute-start.20 = (bf16[2,128,768]{2,1,0:T(8,128)(2,1)}, bf16[2,128,768]{2,1,0:T(8,128)(2,1)}, u32[]{:S(2)}, u32[]{:S(2)}) collective-permute-start(bf16[2,128,768]{2,1,0:T(8,128)(2,1)} %get-tuple-element.104), channel_id=1, source_target_pairs={{0,1},{1,0},{2,3},{3,2},{4,5},{5,4},{6,7},{7,6},{8,9},{9,8},{10,11... | collective-permute-start | bytes 1179656 | tf_op jit(solution)/shard_map/ppermute | solution.py:51
  19.0 27.7 %collective-permute-start.15 = (bf16[1,2,1,1,48,1536]{5,4,3,2,1,0:T(8,128)(2,1)S(1)}, bf16[1,2,1,1,48,1536]{5,4,3,2,1,0:T(8,128)(2,1)S(1)}, u32[]{:S(2)}, u32[]{:S(2)}) collective-permute-start(bf16[1,2,1,1,48,1536]{5,4,3,2,1,0:T(8,128)(2,1)S(1)} %pad_maximum_fusion.24), channel_id=1, source_target_pairs={{0,16},{2,18},{4,20},{6,22},{8,24},{10,26},{12,28},{14,30},{16,0},... | collective-permute-start | bytes 884744 | tf_op jit(solution)/shard_map/ppermute | solution.py:52
  22.7 30.3 %collective-permute-start.10 = (bf16[1,2,1,1,48,1536]{5,4,3,2,1,0:T(8,128)(2,1)S(1)}, bf16[1,2,1,1,48,1536]{5,4,3,2,1,0:T(8,128)(2,1)S(1)}, u32[]{:S(2)}, u32[]{:S(2)}) collective-permute-start(bf16[1,2,1,1,48,1536]{5,4,3,2,1,0:T(8,128)(2,1)S(1)} %pad_maximum_fusion.23), channel_id=1, source_target_pairs={{0,16},{2,18},{4,20},{6,22},{8,24},{10,26},{12,28},{14,30},{16,0},... | collective-permute-start | bytes 884744 | tf_op jit(solution)/shard_map/ppermute | solution.py:52
  23.2 36.6 %collective-permute-start.2 = (bf16[1,2,1,1,48,1664]{5,4,3,2,1,0:T(8,128)(2,1)S(1)}, bf16[1,2,1,1,48,1664]{5,4,3,2,1,0:T(8,128)(2,1)S(1)}, u32[]{:S(2)}, u32[]{:S(2)}) collective-permute-start(bf16[1,2,1,1,48,1664]{5,4,3,2,1,0:T(8,128)(2,1)S(1)} %pad_maximum_fusion.21), channel_id=1, source_target_pairs={{0,16},{2,18},{4,20},{6,22},{8,24},{10,26},{12,28},{14,30},{16,0},... | collective-permute-start | bytes 958472 | tf_op jit(solution)/shard_map/ppermute | solution.py:52
  46.8 27.3 %collective-permute-start.16 = (bf16[2,2,1,1,48,1536]{5,4,3,2,1,0:T(8,128)(2,1)S(1)}, bf16[2,2,1,1,48,1536]{5,4,3,2,1,0:T(8,128)(2,1)S(1)}, u32[]{:S(2)}, u32[]{:S(2)}) collective-permute-start(bf16[2,2,1,1,48,1536]{5,4,3,2,1,0:T(8,128)(2,1)S(1)} %pad_maximum_fusion.20), channel_id=1, source_target_pairs={{0,1},{1,0},{2,3},{3,2},{4,5},{5,4},{6,7},{7,6},{8,9},{9,8},{10,11... | collective-permute-start | bytes 1769480 | tf_op jit(solution)/shard_map/ppermute | solution.py:51
  61.6 20.9 %collective-permute-start.11 = (bf16[2,2,1,1,48,1536]{5,4,3,2,1,0:T(8,128)(2,1)S(1)}, bf16[2,2,1,1,48,1536]{5,4,3,2,1,0:T(8,128)(2,1)S(1)}, u32[]{:S(2)}, u32[]{:S(2)}) collective-permute-start(bf16[2,2,1,1,48,1536]{5,4,3,2,1,0:T(8,128)(2,1)S(1)} %pad_maximum_fusion.19), channel_id=1, source_target_pairs={{0,4},{2,6},{4,0},{6,2},{8,12},{10,14},{12,8},{14,10},{16,20},{18,... | collective-permute-start | bytes 1769480 | tf_op jit(solution)/shard_map/ppermute | solution.py:52
  62.2 10.2 %collective-permute-start.3 = (bf16[2,2,1,1,48,896]{5,4,3,2,1,0:T(8,128)(2,1)S(1)}, bf16[2,2,1,1,48,896]{5,4,3,2,1,0:T(8,128)(2,1)S(1)}, u32[]{:S(2)}, u32[]{:S(2)}) collective-permute-start(bf16[2,2,1,1,48,896]{5,4,3,2,1,0:T(8,128)(2,1)S(1)} %fusion.55), channel_id=1, source_target_pairs={{0,1},{1,0},{2,3},{3,2},{4,5},{5,4},{6,7},{7,6},{8,9},{9,8},{10,11... | collective-permute-start | bytes 1032200 | tf_op jit(solution)/shard_map/ppermute | solution.py:51
  70.0 14.9 %collective-permute-start.7 = (bf16[2,2,2,1,48,768]{5,4,3,2,1,0:T(8,128)(2,1)S(1)}, bf16[2,2,2,1,48,768]{5,4,3,2,1,0:T(8,128)(2,1)S(1)}, u32[]{:S(2)}, u32[]{:S(2)}) collective-permute-start(bf16[2,2,2,1,48,768]{5,4,3,2,1,0:T(8,128)(2,1)S(1)} %pad_maximum_fusion.18), channel_id=1, source_target_pairs={{0,1},{1,0},{2,3},{3,2},{4,5},{5,4},{6,7},{7,6},{8,9},{9,8},{10,11... | collective-permute-start | bytes 1769480 | tf_op jit(solution)/shard_map/ppermute | solution.py:51
  72.5 24.7 %collective-permute-start.4 = (bf16[2,2,1,1,48,1792]{5,4,3,2,1,0:T(8,128)(2,1)S(1)}, bf16[2,2,1,1,48,1792]{5,4,3,2,1,0:T(8,128)(2,1)S(1)}, u32[]{:S(2)}, u32[]{:S(2)}) collective-permute-start(bf16[2,2,1,1,48,1792]{5,4,3,2,1,0:T(8,128)(2,1)S(1)} %pad_maximum_fusion.17), channel_id=1, source_target_pairs={{0,4},{2,6},{4,0},{6,2},{8,12},{10,14},{12,8},{14,10},{16,20},{18,... | collective-permute-start | bytes 2064392 | tf_op jit(solution)/shard_map/ppermute | solution.py:52
  74.3 47.3 %collective-permute-start.17 = (bf16[2,2,1,1,48,3072]{5,4,3,2,1,0:T(8,128)(2,1)S(1)}, bf16[2,2,1,1,48,3072]{5,4,3,2,1,0:T(8,128)(2,1)S(1)}, u32[]{:S(2)}, u32[]{:S(2)}) collective-permute-start(bf16[2,2,1,1,48,3072]{5,4,3,2,1,0:T(8,128)(2,1)S(1)} %pad_maximum_fusion.13), channel_id=1, source_target_pairs={{0,4},{2,6},{4,0},{6,2},{8,12},{10,14},{12,8},{14,10},{16,20},{18,... | collective-permute-start | bytes 3538952 | tf_op jit(solution)/shard_map/ppermute | solution.py:52
  82.7 41.5 %collective-permute-start.12 = (bf16[2,2,2,1,48,1536]{5,4,3,2,1,0:T(8,128)(2,1)S(1)}, bf16[2,2,2,1,48,1536]{5,4,3,2,1,0:T(8,128)(2,1)S(1)}, u32[]{:S(2)}, u32[]{:S(2)}) collective-permute-start(bf16[2,2,2,1,48,1536]{5,4,3,2,1,0:T(8,128)(2,1)S(1)} %pad_maximum_fusion.12), channel_id=1, source_target_pairs={{0,1},{1,0},{2,3},{3,2},{4,5},{5,4},{6,7},{7,6},{8,9},{9,8},{10,11... | collective-permute-start | bytes 3538952 | tf_op jit(solution)/shard_map/ppermute | solution.py:51
  85.1 41.9 %collective-permute-start.8 = (bf16[2,2,2,1,48,1536]{5,4,3,2,1,0:T(8,128)(2,1)S(1)}, bf16[2,2,2,1,48,1536]{5,4,3,2,1,0:T(8,128)(2,1)S(1)}, u32[]{:S(2)}, u32[]{:S(2)}) collective-permute-start(bf16[2,2,2,1,48,1536]{5,4,3,2,1,0:T(8,128)(2,1)S(1)} %pad_maximum_fusion.11), channel_id=1, source_target_pairs={{0,2},{2,0},{4,6},{6,4},{8,10},{10,8},{12,14},{14,12},{16,18},{18,... | collective-permute-start | bytes 3538952 | tf_op jit(solution)/shard_map/ppermute | solution.py:52
  98.8 57.2 %collective-permute-start.5 = (bf16[2,2,2,1,48,1792]{5,4,3,2,1,0:T(8,128)(2,1)}, bf16[2,2,2,1,48,1792]{5,4,3,2,1,0:T(8,128)(2,1)}, u32[]{:S(2)}, u32[]{:S(2)}) collective-permute-start(bf16[2,2,2,1,48,1792]{5,4,3,2,1,0:T(8,128)(2,1)} %pad_maximum_fusion.10), channel_id=1, source_target_pairs={{0,2},{2,0},{4,6},{6,4},{8,10},{10,8},{12,14},{14,12},{16,18},{18,... | collective-permute-start | bytes 4128776 | tf_op jit(solution)/shard_map/ppermute | solution.py:52
  124.2 97.8 %collective-permute-start.18 = (bf16[2,2,2,1,48,3072]{5,4,3,2,1,0:T(8,128)(2,1)}, bf16[2,2,2,1,48,3072]{5,4,3,2,1,0:T(8,128)(2,1)}, u32[]{:S(2)}, u32[]{:S(2)}) collective-permute-start(bf16[2,2,2,1,48,3072]{5,4,3,2,1,0:T(8,128)(2,1)} %pad_maximum_fusion.6), channel_id=1, source_target_pairs={{0,2},{2,0},{4,6},{6,4},{8,10},{10,8},{12,14},{14,12},{16,18},{18,... | collective-permute-start | bytes 7077896 | tf_op jit(solution)/shard_map/ppermute | solution.py:52
  126.5 71.4 %collective-permute-start.13 = (bf16[2,2,2,1,48,3072]{5,4,3,2,1,0:T(8,128)(2,1)}, bf16[2,2,2,1,48,3072]{5,4,3,2,1,0:T(8,128)(2,1)}, u32[]{:S(2)}, u32[]{:S(2)}) collective-permute-start(bf16[2,2,2,1,48,3072]{5,4,3,2,1,0:T(8,128)(2,1)} %pad_maximum_fusion.5), channel_id=1, source_target_pairs={{0,2},{2,0},{4,6},{6,4},{8,10},{10,8},{12,14},{14,12},{16,18},{18,... | collective-permute-start | bytes 7077896 | tf_op jit(solution)/shard_map/ppermute | solution.py:52
  284.2 80.9 %collective-permute-start.19 = (bf16[2,128,768]{2,1,0:T(8,128)(2,1)}, bf16[2,128,768]{2,1,0:T(8,128)(2,1)}, u32[]{:S(2)}, u32[]{:S(2)}) collective-permute-start(bf16[2,128,768]{2,1,0:T(8,128)(2,1)} %slice.225), channel_id=1, source_target_pairs={{0,1},{1,0},{2,3},{3,2},{4,5},{5,4},{6,7},{7,6},{8,9},{9,8},{10,11... | collective-permute-start | bytes 1179656 | tf_op jit(solution)/shard_map/ppermute | solution.py:51
  295.3 91.9 %collective-permute-start.30 = (bf16[2,2,2,1,48,3072]{5,4,3,2,1,0:T(8,128)(2,1)}, bf16[2,2,2,1,48,3072]{5,4,3,2,1,0:T(8,128)(2,1)}, u32[]{:S(2)}, u32[]{:S(2)}) collective-permute-start(bf16[2,2,2,1,48,3072]{5,4,3,2,1,0:T(8,128)(2,1)} %constant_dynamic-slice_fusion.9), channel_id=1, source_target_pairs={{0,2},{2,0},{4,6},{6,4},{8,10},{10,8},{12,14},{14,12},{16,18},{18,... | collective-permute-start | bytes 7077896 | tf_op jit(solution)/shard_map/ppermute | solution.py:52
  341.7 17.7 %collective-permute-start.21 = (bf16[2,128,768]{2,1,0:T(8,128)(2,1)S(1)}, bf16[2,128,768]{2,1,0:T(8,128)(2,1)S(1)}, u32[]{:S(2)}, u32[]{:S(2)}) collective-permute-start(bf16[2,128,768]{2,1,0:T(8,128)(2,1)S(1)} %slice.273), channel_id=1, source_target_pairs={{0,1},{1,0},{2,3},{3,2},{4,5},{5,4},{6,7},{7,6},{8,9},{9,8},{10,11... | collective-permute-start | bytes 1179656 | tf_op jit(solution)/shard_map/ppermute | solution.py:51
  359.4 31.6 %collective-permute-start.35 = (bf16[2,2,2,1,48,3072]{5,4,3,2,1,0:T(8,128)(2,1)S(1)}, bf16[2,2,2,1,48,3072]{5,4,3,2,1,0:T(8,128)(2,1)S(1)}, u32[]{:S(2)}, u32[]{:S(2)}) collective-permute-start(bf16[2,2,2,1,48,3072]{5,4,3,2,1,0:T(8,128)(2,1)S(1)} %constant_dynamic-slice_fusion.4), channel_id=1, source_target_pairs={{0,2},{2,0},{4,6},{6,4},{8,10},{10,8},{12,14},{14,12},{16,18},{18,... | collective-permute-start | bytes 7077896 | tf_op jit(solution)/shard_map/ppermute | solution.py:52
  361.6 15.5 %collective-permute-start.23 = (bf16[2,2,2,1,48,768]{5,4,3,2,1,0:T(8,128)(2,1)S(1)}, bf16[2,2,2,1,48,768]{5,4,3,2,1,0:T(8,128)(2,1)S(1)}, u32[]{:S(2)}, u32[]{:S(2)}) collective-permute-start(bf16[2,2,2,1,48,768]{5,4,3,2,1,0:T(8,128)(2,1)S(1)} %constant_dynamic-slice_fusion.15), channel_id=1, source_target_pairs={{0,1},{1,0},{2,3},{3,2},{4,5},{5,4},{6,7},{7,6},{8,9},{9,8},{10,11... | collective-permute-start | bytes 1769480 | tf_op jit(solution)/shard_map/ppermute | solution.py:51
  363.5 18.4 %collective-permute-start.26 = (bf16[2,2,1,1,48,1792]{5,4,3,2,1,0:T(8,128)(2,1)S(1)}, bf16[2,2,1,1,48,1792]{5,4,3,2,1,0:T(8,128)(2,1)S(1)}, u32[]{:S(2)}, u32[]{:S(2)}) collective-permute-start(bf16[2,2,1,1,48,1792]{5,4,3,2,1,0:T(8,128)(2,1)S(1)} %constant_dynamic-slice_fusion.12), channel_id=1, source_target_pairs={{0,4},{2,6},{4,0},{6,2},{8,12},{10,14},{12,8},{14,10},{16,20},{18,... | collective-permute-start | bytes 2064392 | tf_op jit(solution)/shard_map/ppermute | solution.py:52
  389.3 29.8 %collective-permute-start.31 = (bf16[2,2,1,1,48,3072]{5,4,3,2,1,0:T(8,128)(2,1)S(1)}, bf16[2,2,1,1,48,3072]{5,4,3,2,1,0:T(8,128)(2,1)}, u32[]{:S(2)}, u32[]{:S(2)}) collective-permute-start(bf16[2,2,1,1,48,3072]{5,4,3,2,1,0:T(8,128)(2,1)S(1)} %constant_dynamic-slice_fusion.8), channel_id=1, source_target_pairs={{0,4},{2,6},{4,0},{6,2},{8,12},{10,14},{12,8},{14,10},{16,20},{18,... | collective-permute-start | bytes 3538952 | tf_op jit(solution)/shard_map/ppermute | solution.py:52
  391.0 14.9 %collective-permute-start.28 = (bf16[1,2,1,1,48,1664]{5,4,3,2,1,0:T(8,128)(2,1)S(1)}, bf16[1,2,1,1,48,1664]{5,4,3,2,1,0:T(8,128)(2,1)S(1)}, u32[]{:S(2)}, u32[]{:S(2)}) collective-permute-start(bf16[1,2,1,1,48,1664]{5,4,3,2,1,0:T(8,128)(2,1)S(1)} %fusion.56), channel_id=1, source_target_pairs={{0,16},{2,18},{4,20},{6,22},{8,24},{10,26},{12,28},{14,30},{16,0},... | collective-permute-start | bytes 958472 | tf_op jit(solution)/shard_map/ppermute | solution.py:52
  407.2 29.1 %collective-permute-start.36 = (bf16[2,2,2,1,48,1536]{5,4,3,2,1,0:T(8,128)(2,1)}, bf16[2,2,2,1,48,1536]{5,4,3,2,1,0:T(8,128)(2,1)}, u32[]{:S(2)}, u32[]{:S(2)}) collective-permute-start(bf16[2,2,2,1,48,1536]{5,4,3,2,1,0:T(8,128)(2,1)} %constant_dynamic-slice_fusion.3), channel_id=1, source_target_pairs={{0,1},{1,0},{2,3},{3,2},{4,5},{5,4},{6,7},{7,6},{8,9},{9,8},{10,11... | collective-permute-start | bytes 3538952 | tf_op jit(solution)/shard_map/ppermute | solution.py:51
  420.6 27.3 %collective-permute-start.32 = (bf16[2,2,1,1,48,1536]{5,4,3,2,1,0:T(8,128)(2,1)S(1)}, bf16[2,2,1,1,48,1536]{5,4,3,2,1,0:T(8,128)(2,1)S(1)}, u32[]{:S(2)}, u32[]{:S(2)}) collective-permute-start(bf16[2,2,1,1,48,1536]{5,4,3,2,1,0:T(8,128)(2,1)S(1)} %constant_dynamic-slice_fusion.7), channel_id=1, source_target_pairs={{0,1},{1,0},{2,3},{3,2},{4,5},{5,4},{6,7},{7,6},{8,9},{9,8},{10,11... | collective-permute-start | bytes 1769480 | tf_op jit(solution)/shard_map/ppermute | solution.py:51
  438.1 13.5 %collective-permute-start.37 = (bf16[2,2,1,1,48,1536]{5,4,3,2,1,0:T(8,128)(2,1)S(1)}, bf16[2,2,1,1,48,1536]{5,4,3,2,1,0:T(8,128)(2,1)S(1)}, u32[]{:S(2)}, u32[]{:S(2)}) collective-permute-start(bf16[2,2,1,1,48,1536]{5,4,3,2,1,0:T(8,128)(2,1)S(1)} %constant_dynamic-slice_fusion.2), channel_id=1, source_target_pairs={{0,4},{2,6},{4,0},{6,2},{8,12},{10,14},{12,8},{14,10},{16,20},{18,... | collective-permute-start | bytes 1769480 | tf_op jit(solution)/shard_map/ppermute | solution.py:52
  448.2 22.7 %collective-permute-start.33 = (bf16[1,2,1,1,48,1536]{5,4,3,2,1,0:T(8,128)(2,1)S(1)}, bf16[1,2,1,1,48,1536]{5,4,3,2,1,0:T(8,128)(2,1)S(1)}, u32[]{:S(2)}, u32[]{:S(2)}) collective-permute-start(bf16[1,2,1,1,48,1536]{5,4,3,2,1,0:T(8,128)(2,1)S(1)} %constant_dynamic-slice_fusion.6), channel_id=1, source_target_pairs={{0,16},{2,18},{4,20},{6,22},{8,24},{10,26},{12,28},{14,30},{16,0},... | collective-permute-start | bytes 884744 | tf_op jit(solution)/shard_map/ppermute | solution.py:52
  451.7 24.6 %collective-permute-start.38 = (bf16[1,2,1,1,48,1536]{5,4,3,2,1,0:T(8,128)(2,1)S(1)}, bf16[1,2,1,1,48,1536]{5,4,3,2,1,0:T(8,128)(2,1)S(1)}, u32[]{:S(2)}, u32[]{:S(2)}) collective-permute-start(bf16[1,2,1,1,48,1536]{5,4,3,2,1,0:T(8,128)(2,1)S(1)} %constant_dynamic-slice_fusion.1), channel_id=1, source_target_pairs={{0,16},{2,18},{4,20},{6,22},{8,24},{10,26},{12,28},{14,30},{16,0},... | collective-permute-start | bytes 884744 | tf_op jit(solution)/shard_map/ppermute | solution.py:52
  (87 other events, 1041.3 us)

commit v2 on v1

v2 whole, which is shorter than its diff:
```python
from functools import partial
import math

import jax
import jax.numpy as jnp
from jax import lax
from jax.experimental import pallas as pl
from jax.experimental.pallas import tpu as pltpu
from jax.sharding import PartitionSpec as P

HD = 64
PAIR = 2 * HD
SEQ = 197

norm_epsilon = 1e-06
masked_score = -1e30
f32 = jnp.float32
bf16 = jnp.bfloat16
vmem_limit = 60 * 1024 * 1024


def dot(left, right):
    return jnp.dot(left, right, preferred_element_type=f32)


def dot_nt(left, right):
    return lax.dot_general(left, right, (((1,), (1,)), ((), ())), preferred_element_type=f32)


def dot_tn(left, right):
    return lax.dot_general(left, right, (((0,), (0,)), ((), ())), preferred_element_type=f32)


def mean_of(values):
    return jnp.mean(values, axis=-1, keepdims=True)


def normal_parts(values):
    centre = values - mean_of(values)
    rate = lax.rsqrt(mean_of(centre * centre) + norm_epsilon)
    return centre * rate, rate


def normal_back(normal, rate, norm_gain, grad):
    scaled = grad * norm_gain
    return rate * (scaled - mean_of(scaled) - normal * mean_of(scaled * normal))


def column_sum(values):
    return jnp.sum(values, axis=0, keepdims=True)


def head_masks():
    lane = lax.broadcasted_iota(jnp.int32, (1, PAIR), 1)
    first = (lane < HD).astype(f32)
    return first, 1.0 - first


def both_heads(slab, first, second):
    return jnp.concatenate([slab * first.astype(bf16), slab * second.astype(bf16)], axis=0)


def one_of_each(stacked, first, second):
    size = stacked.shape[0] // 2
    return stacked[:size] * first + stacked[size:] * second


def join_cores(core_ref, own_ref, swapped_ref, whole_ref):
    @pl.when(core_ref[0] == 0)
    def _():
        whole_ref[:, 0] = own_ref[...]
        whole_ref[:, 1] = swapped_ref[...]

    @pl.when(core_ref[0] != 0)
    def _():
        whole_ref[:, 0] = swapped_ref[...]
        whole_ref[:, 1] = own_ref[...]


def flat(value):
    return value.reshape(-1, value.shape[-1])


def split_cores(core_ref, value, kept_ref, sent_ref, columns):
    blocks, rows, _ = kept_ref.shape
    value = value.astype(bf16).reshape(blocks, 2, rows, value.shape[-1])

    @pl.when(core_ref[0] == 0)
    def _():
        kept_ref[:, :, columns] = value[:, 0]
        sent_ref[:, :, columns] = value[:, 1]

    @pl.when(core_ref[0] != 0)
    def _():
        kept_ref[:, :, columns] = value[:, 1]
        sent_ref[:, :, columns] = value[:, 0]


def row_mask(bounds_ref, image, slot_count):
    place = lax.broadcasted_iota(jnp.int32, (slot_count, 1), 0)
    return jnp.concatenate(
        [(place < bounds_ref[image, 2 + part]).astype(f32) for part in range(2)], axis=0
    )


def attend_forward_kernel(
    core_ref,
    bounds_ref,
    own_ref,
    other_ref,
    one_ref,
    one_swapped_ref,
    two_ref,
    two_swapped_ref,
    vec_ref,
    first_ref,
    joint_ref,
    chances_ref,
    mixed_ref,
    middle_ref,
    one_whole,
    two_whole,
):
    image = pl.program_id(0)
    slot_count, width = own_ref.shape[1:]
    half = width // 2

    @pl.when(image == 0)
    def _():
        join_cores(core_ref, one_ref, one_swapped_ref, one_whole)
        join_cores(core_ref, two_ref, two_swapped_ref, two_whole)

    inputs = jnp.concatenate([own_ref[0], other_ref[0]], axis=0).astype(f32)
    normal, _ = normal_parts(inputs)
    first_rows = (normal * vec_ref[0:1] + vec_ref[1:2]).astype(bf16)
    first_ref[0] = first_rows
    for y in range(2):
        at = y * half
        here = slice(at, at + half)
        base = y * 2 * half
        query = dot(first_rows, flat(one_whole[:, :, :, base : base + half])) + vec_ref[6:7, here]
        key = dot(first_rows, flat(one_whole[:, :, :, base + half : base + 2 * half]))
        value = dot(first_rows, flat(two_whole[:, :, :, base : base + half])) + vec_ref[7:8, here]
        joint_ref[0, :, at : at + half] = (query.astype(bf16).astype(f32) * HD ** (-0.5)).astype(bf16)
        joint_ref[0, :, width + at : width + at + half] = key.astype(bf16)
        joint_ref[0, :, 2 * width + at : 2 * width + at + half] = value.astype(bf16)
    place = lax.broadcasted_iota(jnp.int32, (1, slot_count), 1)
    live = jnp.concatenate(
        [(place < bounds_ref[image, part]).astype(jnp.int32) for part in range(2)], axis=1
    )
    first, second = head_masks()
    for pair in range(width // PAIR):
        at = pair * PAIR
        query = both_heads(joint_ref[0, :, at : at + PAIR], first, second)
        key = joint_ref[0, :, width + at : width + at + PAIR]
        value = joint_ref[0, :, 2 * width + at : 2 * width + at + PAIR]
        scores = jnp.where(live > 0, dot_nt(query, key), masked_score)
        raised = jnp.exp(scores - jnp.max(scores, axis=-1, keepdims=True))
        chances = (raised / jnp.sum(raised, axis=-1, keepdims=True)).astype(bf16)
        chances_ref[0, pair] = chances
        mixed_ref[0, :, at : at + PAIR] = one_of_each(dot(chances, value), first, second).astype(
            bf16
        )
    branch = inputs + vec_ref[2:3]
    for y in range(2):
        base = y * 2 * half + half
        branch += dot_nt(
            mixed_ref[0, :, y * half : (y + 1) * half],
            flat(two_whole[:, :, :, base : base + half]),
        )
    middle_ref[0] = branch


def dense_up_kernel(
    core_ref,
    bounds_ref,
    middle_ref,
    own_ref,
    other_ref,
    up_ref,
    up_swapped_ref,
    up_add_ref,
    vec_ref,
    second_ref,
    grad_in_ref,
    active_ref,
    slope_ref,
    kept_ref,
    sent_ref,
    up_whole,
):
    images, slot_count, _ = own_ref.shape
    length = 2 * slot_count

    @pl.when(pl.program_id(0) == 0)
    def _():
        for image in range(images):
            rows = slice(image * length, (image + 1) * length)
            normal, _ = normal_parts(middle_ref[rows])
            second_ref[rows] = (normal * vec_ref[3:4] + vec_ref[4:5]).astype(bf16)
            grads = jnp.concatenate([own_ref[image], other_ref[image]], axis=0).astype(f32)
            grad_in_ref[rows] = (grads * row_mask(bounds_ref, image, slot_count)).astype(bf16)

    join_cores(core_ref, up_ref, up_swapped_ref, up_whole)
    hidden = dot(second_ref[...], flat(up_whole[...])) + up_add_ref[...]
    below = 0.5 * (1.0 + lax.erf(hidden * math.sqrt(0.5)))
    density = jnp.exp(-0.5 * hidden * hidden) * (1.0 / math.sqrt(2.0 * math.pi))
    active = (hidden * below).astype(bf16)
    active_ref[...] = active
    slope_ref[...] = (below + hidden * density).astype(bf16)
    split_cores(core_ref, dot_tn(grad_in_ref[...], active), kept_ref, sent_ref, slice(None))


def dense_down_kernel(
    core_ref,
    bounds_ref,
    middle_ref,
    own_ref,
    other_ref,
    second_ref,
    grad_in_ref,
    active_ref,
    slope_ref,
    up_ref,
    up_swapped_ref,
    down_ref,
    down_swapped_ref,
    vec_ref,
    kept_ref,
    sent_ref,
    up_sums_ref,
    out_own_ref,
    out_other_ref,
    grad_middle_ref,
    sums_ref,
    up_whole,
    down_whole,
    out_total,
    back_total,
):
    step = pl.program_id(0)
    images, slot_count, _ = own_ref.shape
    length = 2 * slot_count
    join_cores(core_ref, up_ref, up_swapped_ref, up_whole)
    join_cores(core_ref, down_ref, down_swapped_ref, down_whole)
    up = flat(up_whole[...])
    down = flat(down_whole[...])
    grad_hidden = (dot(grad_in_ref[...], down) * slope_ref[...].astype(f32)).astype(bf16)
    split_cores(core_ref, dot_tn(second_ref[...], grad_hidden), kept_ref, sent_ref, slice(None))
    up_sums_ref[...] = column_sum(grad_hidden.astype(f32))
    out_part = dot_nt(active_ref[...], down)
    back_part = dot_nt(grad_hidden, up)

    @pl.when(step == 0)
    def _():
        out_total[...] = out_part
        back_total[...] = back_part

    @pl.when(step > 0)
    def _():
        out_total[...] += out_part
        back_total[...] += back_part

    @pl.when(step == pl.num_programs(0) - 1)
    def _():
        sums = [0.0] * 4
        for image in range(images):
            rows = slice(image * length, (image + 1) * length)
            mask = row_mask(bounds_ref, image, slot_count)
            middle = middle_ref[rows]
            result = ((middle + out_total[rows] + vec_ref[5:6]) * mask).astype(bf16)
            out_own_ref[image] = result[:slot_count]
            out_other_ref[image] = result[slot_count:]
            grads = jnp.concatenate([own_ref[image], other_ref[image]], axis=0).astype(f32) * mask
            back = back_total[rows].astype(bf16).astype(f32)
            normal, rate = normal_parts(middle)
            grad_middle = grads + normal_back(normal, rate, vec_ref[3:4], back)
            grad_middle_ref[rows] = grad_middle
            for i, term in enumerate((grad_middle, back * normal, back, grads)):
                sums[i] += column_sum(term)
        for i in range(4):
            sums_ref[i : i + 1] = sums[i]


def attend_backward_kernel(
    core_ref,
    own_ref,
    other_ref,
    grad_middle_ref,
    first_ref,
    joint_ref,
    chances_ref,
    mixed_ref,
    one_ref,
    one_swapped_ref,
    two_ref,
    two_swapped_ref,
    vec_ref,
    one_kept_ref,
    one_sent_ref,
    two_kept_ref,
    two_sent_ref,
    grad_own_ref,
    grad_other_ref,
    sums_ref,
    one_whole,
    two_whole,
    branch_ref,
    grad_joint_ref,
):
    images, slot_count, width = own_ref.shape
    length = 2 * slot_count
    half = width // 2
    join_cores(core_ref, one_ref, one_swapped_ref, one_whole)
    join_cores(core_ref, two_ref, two_swapped_ref, two_whole)
    first, second = head_masks()
    sums = [0.0] * 4
    for image in range(images):
        rows = slice(image * length, (image + 1) * length)
        grad_middle = grad_middle_ref[rows]
        branch = grad_middle.astype(bf16)
        branch_ref[rows] = branch
        grad_mixed = jnp.concatenate(
            [
                dot(branch, flat(two_whole[:, :, :, base : base + half]))
                for base in (half, 3 * half)
            ],
            axis=1,
        ).astype(bf16)
        for pair in range(width // PAIR):
            at = pair * PAIR
            query = both_heads(joint_ref[rows, at : at + PAIR], first, second)
            key = joint_ref[rows, width + at : width + at + PAIR]
            value = joint_ref[rows, 2 * width + at : 2 * width + at + PAIR]
            grad_pair = both_heads(grad_mixed[:, at : at + PAIR], first, second)
            chances = chances_ref[image, pair]
            grad_value = dot_tn(chances, grad_pair)
            wide = chances.astype(f32)
            weighted = wide * dot_nt(grad_pair, value)
            grad_scores = (weighted - wide * jnp.sum(weighted, axis=-1, keepdims=True)).astype(bf16)
            grad_query = one_of_each(dot(grad_scores, key), first, second) * HD ** (-0.5)
            grad_key = dot_tn(grad_scores, query)
            grad_joint_ref[rows, at : at + PAIR] = grad_query.astype(bf16)
            grad_joint_ref[rows, width + at : width + at + PAIR] = grad_key.astype(bf16)
            grad_joint_ref[rows, 2 * width + at : 2 * width + at + PAIR] = grad_value.astype(bf16)
        back = jnp.zeros((length, width), f32)
        for y in range(2):
            at = y * half
            base = y * 2 * half
            for part, matrix in (
                (0, one_whole[:, :, :, base : base + half]),
                (1, one_whole[:, :, :, base + half : base + 2 * half]),
                (2, two_whole[:, :, :, base : base + half]),
            ):
                columns = slice(part * width + at, part * width + at + half)
                back += dot_nt(grad_joint_ref[rows, columns], flat(matrix))
        back = back.astype(bf16).astype(f32)
        inputs = jnp.concatenate([own_ref[image], other_ref[image]], axis=0).astype(f32)
        normal, rate = normal_parts(inputs)
        grad_tokens = grad_middle + normal_back(normal, rate, vec_ref[0:1], back)
        grad_own_ref[image] = grad_tokens[:slot_count]
        grad_other_ref[image] = grad_tokens[slot_count:].astype(bf16)
        sums[0] += column_sum(back * normal)
        sums[1] += column_sum(back)
        sums[2] += column_sum(grad_joint_ref[rows, :width].astype(f32))
        sums[3] += column_sum(grad_joint_ref[rows, 2 * width :].astype(f32))
    for i in range(4):
        sums_ref[i : i + 1] = sums[i]
    first_rows = first_ref[...]
    for y in range(2):
        at = y * half
        base = y * 2 * half
        here = slice(base, base + half)
        after = slice(base + half, base + 2 * half)
        for part, kept, sent, columns in (
            (0, one_kept_ref, one_sent_ref, here),
            (1, one_kept_ref, one_sent_ref, after),
            (2, two_kept_ref, two_sent_ref, here),
        ):
            start = part * width + at
            grad = dot_tn(first_rows, grad_joint_ref[:, start : start + half])
            split_cores(core_ref, grad, kept, sent, columns)
        grad = dot_tn(branch_ref[...], mixed_ref[:, at : at + half])
        split_cores(core_ref, grad, two_kept_ref, two_sent_ref, after)


in_smem = pl.BlockSpec(memory_space=pltpu.SMEM)
in_vmem = pl.BlockSpec(memory_space=pltpu.VMEM)


def fixed(array):
    return pl.BlockSpec(array.shape, lambda *_: (0,) * len(array.shape))


def per_step(shape, axis):
    return pl.BlockSpec(shape, lambda step: tuple(step if i == axis else 0 for i in range(len(shape))))


def params():
    return pltpu.CompilerParams(vmem_limit_bytes=vmem_limit)


def out(shape, kind):
    return jax.ShapeDtypeStruct(shape, kind)


def attend_forward(core, bounds, own, other, one, two, vec):
    images, slot_count, width = own.shape
    length = 2 * slot_count
    pairs = width // PAIR
    blocks, rows, columns = one[0].shape
    row_flops = 2 * width * width * 4 + 4 * length * width * 2
    return pl.pallas_call(
        attend_forward_kernel,
        grid=(images,),
        in_specs=[
            in_smem,
            in_smem,
            per_step((1, slot_count, width), 0),
            per_step((1, slot_count, width), 0),
            *(fixed(array) for array in (*one, *two, vec)),
        ],
        out_specs=[
            per_step((1, length, width), 0),
            per_step((1, length, 3 * width), 0),
            per_step((1, pairs, 2 * length, length), 0),
            per_step((1, length, width), 0),
            per_step((1, length, width), 0),
        ],
        out_shape=[
            out((images, length, width), bf16),
            out((images, length, 3 * width), bf16),
            out((images, pairs, 2 * length, length), bf16),
            out((images, length, width), bf16),
            out((images, length, width), f32),
        ],
        scratch_shapes=[pltpu.VMEM((blocks, 2, rows, columns), bf16)] * 2,
        compiler_params=params(),
        cost_estimate=pl.CostEstimate(
            flops=images * length * row_flops, bytes_accessed=20_000_000, transcendentals=0
        ),
        name="attend_forward",
    )(core, bounds, own, other, *one, *two, vec)


def dense_up(core, bounds, middle, own, other, up, up_add, vec, tile):
    total, width = middle.shape
    blocks, rows, columns = up[0].shape
    weights = per_step((blocks, rows, tile), 2)
    return pl.pallas_call(
        dense_up_kernel,
        grid=(columns // tile,),
        in_specs=[
            in_smem,
            in_smem,
            fixed(middle),
            fixed(own),
            fixed(other),
            weights,
            weights,
            per_step((1, tile), 1),
            fixed(vec),
        ],
        out_specs=[
            pl.BlockSpec((total, width), lambda step: (0, 0)),
            pl.BlockSpec((total, width), lambda step: (0, 0)),
            per_step((total, tile), 1),
            per_step((total, tile), 1),
            weights,
            weights,
        ],
        out_shape=[
            out((total, width), bf16),
            out((total, width), bf16),
            out((total, columns), bf16),
            out((total, columns), bf16),
            out(up[0].shape, bf16),
            out(up[0].shape, bf16),
        ],
        scratch_shapes=[pltpu.VMEM((blocks, 2, rows, tile), bf16)],
        compiler_params=params(),
        cost_estimate=pl.CostEstimate(
            flops=total * width * columns * 4, bytes_accessed=20_000_000, transcendentals=0
        ),
        name="dense_up",
    )(core, bounds, middle, own, other, *up, up_add, vec)


def dense_down(
    core, bounds, middle, own, other, second, grad_in, active, slope, up, down, vec, tile
):
    total, width = middle.shape
    blocks, rows, columns = up[0].shape
    weights = per_step((blocks, rows, tile), 2)
    whole = pl.BlockSpec((total, width), lambda step: (0, 0))
    return pl.pallas_call(
        dense_down_kernel,
        grid=(columns // tile,),
        in_specs=[
            in_smem,
            in_smem,
            whole,
            fixed(own),
            fixed(other),
            whole,
            whole,
            per_step((total, tile), 1),
            per_step((total, tile), 1),
            weights,
            weights,
            weights,
            weights,
            fixed(vec),
        ],
        out_specs=[
            weights,
            weights,
            per_step((1, tile), 1),
            fixed(own),
            fixed(own),
            whole,
            pl.BlockSpec((8, width), lambda step: (0, 0)),
        ],
        out_shape=[
            out(up[0].shape, bf16),
            out(up[0].shape, bf16),
            out((1, columns), f32),
            out(own.shape, bf16),
            out(own.shape, bf16),
            out((total, width), f32),
            out((8, width), f32),
        ],
        scratch_shapes=[
            pltpu.VMEM((blocks, 2, rows, tile), bf16),
            pltpu.VMEM((blocks, 2, rows, tile), bf16),
            pltpu.VMEM((total, width), f32),
            pltpu.VMEM((total, width), f32),
        ],
        compiler_params=params(),
        cost_estimate=pl.CostEstimate(
            flops=total * width * columns * 8, bytes_accessed=20_000_000, transcendentals=0
        ),
        name="dense_down",
    )(
        core, bounds, middle, own, other, second, grad_in, active, slope, *up, *down, vec
    )


def attend_backward(core, own, other, grad_middle, first_rows, joint, chances, mixed, one, two, vec):
    images, slot_count, width = own.shape
    total = 2 * images * slot_count
    shape = one[0].shape
    blocks, rows, columns = shape
    return pl.pallas_call(
        attend_backward_kernel,
        in_specs=[in_smem] + [in_vmem] * 12,
        out_specs=[in_vmem] * 7,
        out_shape=[
            out(shape, bf16),
            out(shape, bf16),
            out(shape, bf16),
            out(shape, bf16),
            out(own.shape, f32),
            out(own.shape, bf16),
            out((8, width), f32),
        ],
        scratch_shapes=[
            pltpu.VMEM((blocks, 2, rows, columns), bf16),
            pltpu.VMEM((blocks, 2, rows, columns), bf16),
            pltpu.VMEM((total, width), bf16),
            pltpu.VMEM((total, 3 * width), bf16),
        ],
        compiler_params=params(),
        cost_estimate=pl.CostEstimate(
            flops=total * width * width * 18, bytes_accessed=20_000_000, transcendentals=0
        ),
        name="attend_backward",
    )(core, own, other, grad_middle, first_rows, joint, chances, mixed, *one, *two, vec)


class Exchange:
    def __init__(self, fsdp, tp):
        self.fsdp = fsdp
        self.tp = tp
        self.bits = fsdp.bit_length() - 1
        self.f = lax.axis_index("fsdp")
        self.y = lax.axis_index("tp")

    def side(self, bit):
        return self.y if bit == "y" else (self.f >> bit) & 1

    def swap(self, value, bit):
        if bit == "y":
            return lax.ppermute(value, "tp", [(0, 1), (1, 0)])
        return lax.ppermute(value, "fsdp", [(i, i ^ (1 << bit)) for i in range(self.fsdp)])

    def axis(self, bit):
        return self.bits + 1 if bit == "y" else self.bits - 1 - bit

    def spread_once(self, value, bit):
        other = self.swap(value, bit)
        first = self.side(bit) == 0
        return jnp.concatenate(
            [jnp.where(first, value, other), jnp.where(first, other, value)], axis=self.axis(bit)
        )

    def fold_once(self, value, bit):
        axis = self.axis(bit)
        size = value.shape[axis] // 2
        side = self.side(bit)
        sent = lax.dynamic_slice_in_dim(value, (1 - side) * size, size, axis)
        kept = lax.dynamic_slice_in_dim(value, side * size, size, axis)
        return kept + self.swap(sent, bit)

    def far_bits(self):
        return list(range(2, self.bits))

    def spread(self, value, order):
        for bit in order:
            value = self.spread_once(value, bit)
        return value

    def fold(self, value, order):
        for bit in order:
            value = self.fold_once(value, bit)
        return value

    def cores_apart(self, rows):
        return rows % 16 == 0

    def spread_pair(self, value, order):
        value = self.spread(value, order)
        rows, columns = value.shape[-2:]
        if self.cores_apart(rows):
            pair = value, self.swap(value, 0)
            return tuple(part.reshape(-1, rows, columns) for part in pair)
        value = self.whole(self.spread_once(value, 0))
        size = value.shape[0] // 2
        return value[None, :size], value[None, size:]

    def core(self, rows):
        return (self.side(0) if self.cores_apart(rows) else jnp.zeros((), jnp.int32)).reshape(1)

    def fold_pair(self, kept, sent, rows, order):
        if self.cores_apart(rows):
            value = kept + self.swap(sent, 0)
            value = value.reshape((2,) * (self.bits - 1) + (1, rows, kept.shape[-1]))
            return self.fold(value, order)
        whole = jnp.concatenate([kept[0], sent[0]], axis=0)
        return self.fold(self.cut(whole), [0] + order)

    def opened(self, shard):
        return shard.reshape((1,) * self.bits + shard.shape)

    def whole(self, gathered):
        return gathered.reshape(-1, gathered.shape[-1])

    def cut(self, whole):
        rows, columns = whole.shape
        return whole.reshape((2,) * self.bits + (rows // self.fsdp, columns))


def on_device(
    fsdp,
    tp,
    tokens,
    cotangent,
    image_counts,
    split_points,
    attend_gain,
    attend_shift,
    qkv_weight,
    query_value_bias,
    output_weight,
    output_bias,
    dense_gain,
    dense_shift,
    up_weight,
    up_bias,
    down_weight,
    down_bias,
):
    ex = Exchange(fsdp, tp)
    y = ex.y
    slots, slot_count, width = tokens.shape
    images = slots // 2
    rows = width // fsdp
    half = output_weight.shape[0]
    far = ex.far_bits()
    back_far = far[::-1]
    total = images * 2 * slot_count
    core = ex.core(rows)

    def take(array, start):
        return lax.dynamic_slice_in_dim(array, start, images, 0)

    def rows_of(array):
        return take(array, y * images), ex.swap(take(array, (1 - y) * images), "y")

    def rows_back(own, other):
        back = ex.swap(other, "y").astype(own.dtype)
        first = y == 0
        return jnp.concatenate([jnp.where(first, own, back), jnp.where(first, back, own)], axis=0)

    points = take(split_points, y * images)
    own_bound = jnp.where(y == 0, points, SEQ - points)
    bounds = jnp.stack([own_bound, SEQ - own_bound], axis=1)
    live_images = y * images + jnp.arange(images) < image_counts[0]
    bounds = jnp.concatenate([bounds, jnp.where(live_images[:, None], bounds, 0)], axis=1)

    small = jnp.concatenate(
        [
            attend_gain,
            attend_shift,
            output_bias,
            dense_gain,
            dense_shift,
            down_bias,
            query_value_bias.reshape(-1),
            up_bias,
        ]
    )
    small_size = small.shape[0]
    small_room = -(-small_size // 128) * 128
    small = jnp.pad(small, (0, small_room - small_size)).reshape(1, small_room)
    attend_shard = jnp.concatenate([qkv_weight.reshape(rows, 3 * half), output_weight.T], axis=1)
    token_rows = rows_of(tokens)
    attend_far = ex.spread(ex.opened(attend_shard), far)
    one = ex.spread_pair(attend_far[..., : 2 * half], [1, "y"])
    two = ex.spread_pair(attend_far[..., 2 * half :], ["y", 1])
    small_all = ex.whole(ex.spread(ex.opened(small), far + [1, "y", 0]))
    up = ex.spread_pair(ex.opened(up_weight), far + [1, "y"])
    down = ex.spread_pair(ex.opened(down_weight.T), far + ["y", 1])
    grad_rows = rows_of(cotangent)

    short = rows // 2
    small_all = small_all.reshape(fsdp, 2, small_room).astype(f32)
    plain = small_all[:, 0, : 6 * rows].reshape(fsdp, 6, rows).transpose(1, 0, 2).reshape(6, width)
    joint_add = small_all[:, :, 6 * rows : 7 * rows].reshape(fsdp, 2, 2, short)
    joint_add = joint_add.transpose(2, 1, 0, 3).reshape(2, width)
    vec = jnp.concatenate([plain, joint_add], axis=0)
    up_add = small_all[:, :, 7 * rows : 9 * rows].transpose(1, 0, 2).reshape(1, -1)

    tile = math.gcd(up_add.shape[1], 512)
    first_rows, joint, chances, mixed, middle = attend_forward(
        core, bounds, *token_rows, one, two, vec
    )
    middle = middle.reshape(total, width)
    second, grad_in, active, slope, down_kept, down_sent = dense_up(
        core, bounds, middle, *grad_rows, up, up_add, vec, tile
    )
    grad_down = ex.fold_pair(down_kept, down_sent, rows, ["y", 1] + back_far)
    up_kept, up_sent, up_sums, out_own, out_other, grad_middle, dense_sums = dense_down(
        core, bounds, middle, *grad_rows, second, grad_in, active, slope, up, down, vec, tile
    )
    grad_up = ex.fold_pair(up_kept, up_sent, rows, [1, "y"] + back_far)
    out_tokens = rows_back(out_own, out_other)
    one_kept, one_sent, two_kept, two_sent, grad_own, grad_other, attend_sums = attend_backward(
        core,
        *token_rows,
        grad_middle,
        first_rows.reshape(total, width),
        joint.reshape(total, 3 * width),
        chances,
        mixed.reshape(total, width),
        one,
        two,
        vec,
    )
    grad_tokens = rows_back(grad_own, grad_other)

    plain_grads = jnp.concatenate([attend_sums[:2], dense_sums[:4]], axis=0)
    plain_grads = plain_grads.reshape(6, fsdp, rows).transpose(1, 0, 2).reshape(fsdp, 1, 6 * rows)
    plain_grads = jnp.broadcast_to(plain_grads, (fsdp, 2, 6 * rows))
    bias_grads = attend_sums[2:4].reshape(2, 2, fsdp, short).transpose(2, 1, 0, 3)
    bias_grads = bias_grads.reshape(fsdp, 2, rows)
    up_grads = up_sums.reshape(2, fsdp, 2 * rows).transpose(1, 0, 2)
    small_grads = jnp.concatenate([plain_grads, bias_grads, up_grads], axis=-1)
    small_grads = jnp.pad(small_grads, ((0, 0), (0, 0), (0, small_room - small_size)))
    small_home = ex.fold(ex.cut(small_grads.reshape(fsdp, -1)), [0, 1, "y"] + back_far)
    small_home = small_home.reshape(-1)
    part_one = ex.fold_pair(one_kept, one_sent, rows, ["y", 1])
    part_two = ex.fold_pair(two_kept, two_sent, rows, [1, "y"])
    attend_grads = ex.fold(jnp.concatenate([part_one, part_two], axis=-1), back_far)
    attend_grads = ex.whole(attend_grads)
    grad_qkv = attend_grads[:, : 3 * half].astype(f32).reshape(rows, 3, half)
    grad_output = attend_grads[:, 3 * half :].astype(f32).T
    plain_home = small_home[: 6 * rows].reshape(6, rows)
    return (
        out_tokens,
        grad_tokens,
        plain_home[0],
        plain_home[1],
        grad_qkv,
        small_home[6 * rows : 7 * rows].reshape(2, short),
        grad_output,
        plain_home[2],
        plain_home[3],
        plain_home[4],
        ex.whole(grad_up).astype(f32),
        small_home[7 * rows : 9 * rows],
        ex.whole(grad_down).astype(f32).T,
        plain_home[5],
    )


def solution(mesh):
    return jax.shard_map(
        partial(on_device, mesh.shape["fsdp"], mesh.shape["tp"]),
        mesh=mesh,
        in_specs=(
            P("fsdp", "tp", None),
            P("fsdp", "tp", None),
            P("fsdp"),
            P("fsdp"),
            P("fsdp"),
            P("fsdp"),
            P("fsdp", None, "tp"),
            P(None, ("tp", "fsdp")),
            P("tp", "fsdp"),
            P("fsdp"),
            P("fsdp"),
            P("fsdp"),
            P("fsdp", "tp"),
            P(("tp", "fsdp")),
            P("tp", "fsdp"),
            P("fsdp"),
        ),
        out_specs=(
            P("fsdp", "tp", None),
            P("fsdp", "tp", None),
            P("fsdp"),
            P("fsdp"),
            P("fsdp", None, "tp"),
            P(None, ("tp", "fsdp")),
            P("tp", "fsdp"),
            P("fsdp"),
            P("fsdp"),
            P("fsdp"),
            P("fsdp", "tp"),
            P(("tp", "fsdp")),
            P("tp", "fsdp"),
            P("fsdp"),
        ),
        check_vma=False,
    )
```

time: 491 us -> 373 us (0.76)
  matrix products: 80.7 us -> 0 us
  local copies, waits for them, and re-layouts: 114 us -> 33.6 us
  Pallas kernels: 0 us -> 71.6 us
  other arithmetic: 75.5 us -> 27.8 us
  waiting for transfers between devices: 170 us -> 182 us
  starting transfers between devices: 40.5 us -> 48.8 us
    dot_general x17 -> x0, matrix products: 74.4 us -> none  [the longest x1 8.06 us: on_device(): jnp.einsum('gsd,df->gsf', grad_down_in, down_whole, preferred_element_typ...]
    pallas_call x0 -> x4, Pallas kernels: none -> 71.6 us  [the longest x1 23.2 us: attend_backward(): pl.pallas_call(attend_backward_kernel, in_specs=[in_smem] + [in_vmem] * 1...]
    ppermute x12 -> x14, waiting for transfers between devices: 35.4 us -> 68.2 us  [swap(): return lax.ppermute(value, 'tp', [(0, 1), (1, 0)])]
    slice x20 -> x6, local copies, waits for them, and re-layouts: 27.7 us -> 4.99 us  [the longest x2 2.13 us: on_device(): joint_add = small_all[:, :, 6 * rows:7 * rows].reshape(fsdp, 2, 2, short)]
    convert_element_type x8 -> x1, other arithmetic: 23 us -> 0.71 us  [on_device(): small_all = small_all.reshape(fsdp, 2, small_room).astype(f32)]
    ppermute x28 -> x36, waiting for transfers between devices: 134 us -> 114 us  [swap(): lax.ppermute(value, 'fsdp', [(i, i ^ 1 << bit) for i in range(self.fsdp)])]
    another operation x13 -> x2, local copies, waits for them, and re-layouts: 20 us -> 1.45 us  [the longest x1 1.44 us: on_device(): small_all[:, 0, :6 * rows].reshape(fsdp, 6, rows).transpose(1, 0, 2)]
    reshape x13 -> x12, local copies, waits for them, and re-layouts: 19.1 us -> 5.36 us  [the longest x1 1.49 us: on_device(): small_all[:, 0, :6 * rows].reshape(fsdp, 6, rows).transpose(1, 0, 2)]
  transfers between devices with their start and end apart: 40 -> 50, of which waited for: 22 -> 26; matrix products, arithmetic and copies ran while one was open for 42% -> 14% of each run, Pallas kernels for 0% -> 7%
where the time goes in v2:
time: 373 us; the launch traced here: 367 us
  waiting for transfers between devices  182 us (49%)
  Pallas kernels  71.6 us (19%)
  starting transfers between devices  48.8 us (13%)
  local copies, waits for them, and re-layouts  33.6 us (9%)
  other arithmetic  27.8 us (7%)
    ppermute x36, waiting for transfers between devices, swap(): lax.ppermute(value, 'fsdp', [(i, i ^ 1 << bit) for i in range(self.fsdp)])  114 us
    ppermute x14, waiting for transfers between devices, swap(): return lax.ppermute(value, 'tp', [(0, 1), (1, 0)])  68.2 us
    ppermute x36, starting transfers between devices, swap(): lax.ppermute(value, 'fsdp', [(i, i ^ 1 << bit) for i in range(self.fsdp)])  35.8 us
    pallas_call x1, Pallas kernels, attend_backward(): pl.pallas_call(attend_backward_kernel, in_specs=[in_smem] + [in_vmem] * 1...  23.2 us
    pallas_call x1, Pallas kernels, dense_down(): pl.pallas_call(dense_down_kernel, grid=(columns // tile,), in_specs=[in_s...  22.3 us
    pallas_call x1, Pallas kernels, dense_up(): pl.pallas_call(dense_up_kernel, grid=(columns // tile,), in_specs=[in_sme...  14.3 us
    ppermute x14, starting transfers between devices, swap(): return lax.ppermute(value, 'tp', [(0, 1), (1, 0)])  13 us
    pallas_call x1, Pallas kernels, attend_forward(): pl.pallas_call(attend_forward_kernel, grid=(images,), in_specs=[in_smem,...  11.8 us
  transfers between devices with their start and end apart: 50, of which 26 were waited for; matrix products, arithmetic and copies ran while one was open for 14% of the time, Pallas kernels for 7%

profile of v2, /device:TPU:0, one launch (start us, length us, event | category | flops | bytes accessed | tf_op | source)
XLA Modules:
  0.0 366.6 jit_solution(13170277554155639112)
XLA Ops:
  2.4 3.1 collective-permute-start.1
  6.3 4.8 %concatenate.93 = bf16[432]{0:T(512)(128)(2,1)S(1)} concatenate(bf16[48]{0:T(256)(128)(2,1)} %param.20, bf16[48]{0:T(256)(128)(2,1)} %param.21, bf16[48]{0:T(256)(128)(2,1)} %param.25, bf16[48]{0:T(256)(128)(2,1)} %param.26, bf16[48]{0:T(256)(128)(2,1)} %param.27, bf16[48]{0:T(256)(128)(2,1)} %param.31, bf16[48]{0:T(256)(128)(2,1)S(1)} %reshape.171, bf16[96]{0:T(256)(128)(2,1)} %param.29), dimensions={0} | concatenate | bytes 1728 | tf_op jit(solution)/shard_map/concatenate | solution.py:711
  15.5 3.0 collective-permute-start.10
  26.1 2.5 collective-permute-start.16
  29.3 2.5 collective-permute-start.21
  31.8 21.3 %collective-permute-done.16 = bf16[1,2,1,1,48,1536]{5,4,3,2,1,0:T(8,128)(2,1)S(1)} collective-permute-done((bf16[1,2,1,1,48,1536]{5,4,3,2,1,0:T(8,128)(2,1)S(1)}, bf16[1,2,1,1,48,1536]{5,4,3,2,1,0:T(8,128)(2,1)S(1)}, u32[]{:S(2)}, u32[]{:S(2)}) %collective-permute-start.16) | collective-permute-done | bytes 294944 | tf_op jit(solution)/shard_map/ppermute | solution.py:595
  54.8 4.7 %collective-permute-done.2 = bf16[1,2,1,1,48,1536]{5,4,3,2,1,0:T(8,128)(2,1)S(1)} collective-permute-done((bf16[1,2,1,1,48,1536]{5,4,3,2,1,0:T(8,128)(2,1)S(1)}, bf16[1,2,1,1,48,1536]{5,4,3,2,1,0:T(8,128)(2,1)S(1)}, u32[]{:S(2)}, u32[]{:S(2)}) %collective-permute-start.2) | collective-permute-done | bytes 294944 | tf_op jit(solution)/shard_map/ppermute | solution.py:595
  61.6 3.0 collective-permute-done.21
  68.0 7.9 %collective-permute-done.3 = bf16[2,2,1,1,48,768]{5,4,3,2,1,0:T(8,128)(2,1)S(1)} collective-permute-done((bf16[2,2,1,1,48,768]{5,4,3,2,1,0:T(8,128)(2,1)S(1)}, bf16[2,2,1,1,48,768]{5,4,3,2,1,0:T(8,128)(2,1)S(1)}, u32[]{:S(2)}, u32[]{:S(2)}) %collective-permute-start.3) | collective-permute-done | bytes 294944 | tf_op jit(solution)/shard_map/ppermute | solution.py:595
  78.4 2.6 collective-permute-done.22
  82.8 5.7 %collective-permute-done.7 = bf16[2,2,1,1,48,1536]{5,4,3,2,1,0:T(8,128)(2,1)S(1)} collective-permute-done((bf16[2,2,1,1,48,1536]{5,4,3,2,1,0:T(8,128)(2,1)S(1)}, bf16[2,2,1,1,48,1536]{5,4,3,2,1,0:T(8,128)(2,1)S(1)}, u32[]{:S(2)}, u32[]{:S(2)}) %collective-permute-start.7) | collective-permute-done | bytes 589856 | tf_op jit(solution)/shard_map/ppermute | solution.py:595
  89.0 27.9 %collective-permute-done.18 = bf16[2,2,2,1,48,1536]{5,4,3,2,1,0:T(8,128)(2,1)S(1)} collective-permute-done((bf16[2,2,2,1,48,1536]{5,4,3,2,1,0:T(8,128)(2,1)S(1)}, bf16[2,2,2,1,48,1536]{5,4,3,2,1,0:T(8,128)(2,1)S(1)}, u32[]{:S(2)}, u32[]{:S(2)}) %collective-permute-start.18) | collective-permute-done | bytes 1179680 | tf_op jit(solution)/shard_map/ppermute | solution.py:594
  124.2 3.3 collective-permute-done.13
  147.0 11.8 %attend_forward.1 = (bf16[2,256,768]{2,1,0:T(8,128)(2,1)}, bf16[2,256,2304]{2,1,0:T(8,128)(2,1)}, bf16[2,6,512,256]{3,2,1,0:T(8,128)(2,1)}, bf16[2,256,768]{2,1,0:T(8,128)(2,1)}, f32[2,256,768]{2,1,0:T(8,128)}) custom-call(s32[1]{0:T(128)} %bitcast.core_ref, s32[2,4]{1,0:T(2,128)} %pad_add_fusion.bounds_ref, bf16[2,128,768]{2,1,0:T(8,128)(2,1)} %get-tuple-element.99.own_ref, ...), custom_call_target="tpu_custom_call" | custom-call | flops 3221225472 | bytes 20000000 | tf_op jit(solution)/shard_map/attend_forward/pallas_call | solution.py:413
  159.5 14.3 %dense_up.1 = (bf16[512,768]{1,0:T(8,128)(2,1)}, bf16[512,768]{1,0:T(8,128)(2,1)}, bf16[512,3072]{1,0:T(8,128)(2,1)}, bf16[512,3072]{1,0:T(8,128)(2,1)}, bf16[8,...) custom-call(s32[1]{0:T(128)} %bitcast.core_ref, s32[2,4]{1,0:T(2,128)} %pad_add_fusion.bounds_ref, ...), custom_call_target="tpu_custom_call" | custom-call | flops 4831838208 | bytes 20000000 | tf_op jit(solution)/shard_map/dense_up/pallas_call | solution.py:450
  173.8 22.3 %dense_down.1 = (bf16[8,48,3072]{2,1,0:T(8,128)(2,1)}, bf16[8,48,3072]{2,1,0:T(8,128)(2,1)}, f32[1,3072]{1,0:T(1,128)}, bf16[2,128,768]{2,1,0:T(8,128)(2,1)}, bf...) custom-call(s32[1]{0:T(128)} %bitcast.core_ref, s32[2,4]{1,0:T(2,128)} %pad_add_fusion.bounds_ref, ...), custom_call_target="tpu_custom_call" | custom-call | flops 9663676416 | bytes 20000000 | tf_op jit(solution)/shard_map/dense_down/pallas_call | solution.py:496
  196.2 23.2 %attend_backward.1 = (bf16[8,48,1536]{2,1,0:T(8,128)(2,1)}, bf16[8,48,1536]{2,1,0:T(8,128)(2,1)}, bf16[8,48,1536]{2,1,0:T(8,128)(2,1)}, bf16[8,48,1536]{2,1,0:T(...) custom-call(s32[1]{0:T(128)} %bitcast.core_ref, ...), custom_call_target="tpu_custom_call" | custom-call | flops 5435817984 | bytes 20000000 | tf_op jit(solution)/shard_map/attend_backward/pallas_call | solution.py:554
  225.2 2.2 collective-permute-done.28
  228.0 3.1 collective-permute-done.29
  231.9 3.8 %collective-permute-done.30 = f32[1,2,1,1,1,512]{5,4,3,2,1,0:T(1,128)S(1)} collective-permute-done((f32[1,2,1,1,1,512]{5,4,3,2,1,0:T(1,128)S(1)}, f32[1,2,1,1,1,512]{5,4,3,2,1,0:T(1,128)S(1)}, u32[]{:S(2)}, u32[]{:S(2)}) %collective-permute-start.30) | collective-permute-done | bytes 4128 | tf_op jit(solution)/shard_map/ppermute | solution.py:595
  247.2 7.6 %collective-permute-done.36 = bf16[2,2,1,1,48,1536]{5,4,3,2,1,0:T(8,128)(2,1)} collective-permute-done((bf16[2,2,1,1,48,1536]{5,4,3,2,1,0:T(8,128)(2,1)}, bf16[2,2,1,1,48,1536]{5,4,3,2,1,0:T(8,128)(2,1)}, u32[]{:S(2)}, u32[]{:S(2)}) %collective-permute-start.36) | collective-permute-done | bytes 589856 | tf_op jit(solution)/shard_map/ppermute | solution.py:595
  257.5 10.8 %collective-permute-done.33 = bf16[2,2,2,1,48,768]{5,4,3,2,1,0:T(8,128)(2,1)S(1)} collective-permute-done((bf16[2,2,2,1,48,768]{5,4,3,2,1,0:T(8,128)(2,1)S(1)}, bf16[2,2,2,1,48,768]{5,4,3,2,1,0:T(8,128)(2,1)S(1)}, u32[]{:S(2)}, u32[]{:S(2)}) %collective-permute-start.33) | collective-permute-done | bytes 589856 | tf_op jit(solution)/shard_map/ppermute | solution.py:594
  272.7 2.3 collective-permute-done.37
  279.3 9.4 %collective-permute-done.38 = bf16[1,2,1,1,48,1536]{5,4,3,2,1,0:T(8,128)(2,1)S(1)} collective-permute-done((bf16[1,2,1,1,48,1536]{5,4,3,2,1,0:T(8,128)(2,1)S(1)}, bf16[1,2,1,1,48,1536]{5,4,3,2,1,0:T(8,128)(2,1)S(1)}, u32[]{:S(2)}, u32[]{:S(2)}) %collective-permute-start.38) | collective-permute-done | bytes 294944 | tf_op jit(solution)/shard_map/ppermute | solution.py:595
  288.9 2.6 add.198
  297.1 20.3 %collective-permute-done.46 = bf16[2,2,2,1,48,1536]{5,4,3,2,1,0:T(8,128)(2,1)S(1)} collective-permute-done((bf16[2,2,2,1,48,1536]{5,4,3,2,1,0:T(8,128)(2,1)S(1)}, bf16[2,2,2,1,48,1536]{5,4,3,2,1,0:T(8,128)(2,1)S(1)}, u32[]{:S(2)}, u32[]{:S(2)}) %collective-permute-start.46) | collective-permute-done | bytes 1179680 | tf_op jit(solution)/shard_map/ppermute | solution.py:594
  319.3 3.1 collective-permute-done.41
  322.8 9.7 %collective-permute-done.47 = bf16[2,2,1,1,48,1536]{5,4,3,2,1,0:T(8,128)(2,1)S(1)} collective-permute-done((bf16[2,2,1,1,48,1536]{5,4,3,2,1,0:T(8,128)(2,1)S(1)}, bf16[2,2,1,1,48,1536]{5,4,3,2,1,0:T(8,128)(2,1)S(1)}, u32[]{:S(2)}, u32[]{:S(2)}) %collective-permute-start.47) | collective-permute-done | bytes 589856 | tf_op jit(solution)/shard_map/ppermute | solution.py:595
  335.9 17.9 %collective-permute-done.48 = bf16[1,2,1,1,48,1536]{5,4,3,2,1,0:T(8,128)(2,1)S(1)} collective-permute-done((bf16[1,2,1,1,48,1536]{5,4,3,2,1,0:T(8,128)(2,1)S(1)}, bf16[1,2,1,1,48,1536]{5,4,3,2,1,0:T(8,128)(2,1)S(1)}, u32[]{:S(2)}, u32[]{:S(2)}) %collective-permute-start.48) | collective-permute-done | bytes 294944 | tf_op jit(solution)/shard_map/ppermute | solution.py:595
  354.0 5.2 %collective-permute-done.43 = bf16[1,2,1,1,48,1536]{5,4,3,2,1,0:T(8,128)(2,1)S(1)} collective-permute-done((bf16[1,2,1,1,48,1536]{5,4,3,2,1,0:T(8,128)(2,1)S(1)}, bf16[1,2,1,1,48,1536]{5,4,3,2,1,0:T(8,128)(2,1)S(1)}, u32[]{:S(2)}, u32[]{:S(2)}) %collective-permute-start.43) | collective-permute-done | bytes 294944 | tf_op jit(solution)/shard_map/ppermute | solution.py:595
  359.3 3.0 collective-permute-done.49
  363.1 2.3 collective-permute-done.44
  (246 shorter events, 96.5 us)
Async XLA Ops:
  2.4 23.5 %collective-permute-start.1 = (bf16[1,1,1,1,48,1536]{5,4,3,2,1,0:T(8,128)(2,1)S(1)}, bf16[1,1,1,1,48,1536]{5,4,3,2,1,0:T(8,128)(2,1)S(1)}, u32[]{:S(2)}, u32[]{:S(2)}) collective-permute-start(bf16[1,1,1,1,48,1536]{5,4,3,2,1,0:T(8,128)(2,1)S(1)} %maximum_bitcast_fusion), channel_id=1, source_target_pairs={{0,8},{2,10},{4,12},{6,14},{8,0},{10,2},{12,4},{14,6},{16,24},{18,... | collective-permute-start | bytes 442376 | tf_op jit(solution)/shard_map/ppermute | solution.py:595
  5.5 20.4 %collective-permute-start.15 = (bf16[1,1,1,1,48,1536]{5,4,3,2,1,0:T(8,128)(2,1)}, bf16[1,1,1,1,48,1536]{5,4,3,2,1,0:T(8,128)(2,1)S(1)}, u32[]{:S(2)}, u32[]{:S(2)}) collective-permute-start(bf16[1,1,1,1,48,1536]{5,4,3,2,1,0:T(8,128)(2,1)} %bitcast.116), channel_id=1, source_target_pairs={{0,8},{2,10},{4,12},{6,14},{8,0},{10,2},{12,4},{14,6},{16,24},{18,... | collective-permute-start | bytes 442376 | tf_op jit(solution)/shard_map/ppermute | solution.py:595
  13.1 16.1 %collective-permute-start.20 = (bf16[1,1,1,1,48,1536]{5,4,3,2,1,0:T(8,128)(2,1)}, bf16[1,1,1,1,48,1536]{5,4,3,2,1,0:T(8,128)(2,1)S(1)}, u32[]{:S(2)}, u32[]{:S(2)}) collective-permute-start(bf16[1,1,1,1,48,1536]{5,4,3,2,1,0:T(8,128)(2,1)} %bitcast.117), channel_id=1, source_target_pairs={{0,8},{2,10},{4,12},{6,14},{8,0},{10,2},{12,4},{14,6},{16,24},{18,... | collective-permute-start | bytes 442376 | tf_op jit(solution)/shard_map/ppermute | solution.py:595
  24.4 97.8 %collective-permute-start.12 = (bf16[2,2,2,1,1,512]{5,3,2,1,0,4:T(2,128)(2,1)S(1)}, bf16[2,2,2,1,1,512]{5,3,2,1,0,4:T(2,128)(2,1)S(1)}, u32[]{:S(2)}, u32[]{:S(2)}) collective-permute-start(bf16[2,2,2,1,1,512]{5,3,2,1,0,4:T(2,128)(2,1)S(1)} %pad_maximum_fusion.19), channel_id=1, source_target_pairs={{0,1},{1,0},{2,3},{3,2},{4,5},{5,4},{6,7},{7,6},{8,9},{9,8},{10,11... | collective-permute-start | bytes 24584 | tf_op jit(solution)/shard_map/ppermute | solution.py:594
  26.1 27.0 %collective-permute-start.16 = (bf16[1,2,1,1,48,1536]{5,4,3,2,1,0:T(8,128)(2,1)S(1)}, bf16[1,2,1,1,48,1536]{5,4,3,2,1,0:T(8,128)(2,1)S(1)}, u32[]{:S(2)}, u32[]{:S(2)}) collective-permute-start(bf16[1,2,1,1,48,1536]{5,4,3,2,1,0:T(8,128)(2,1)S(1)} %pad_maximum_fusion.14), channel_id=1, source_target_pairs={{0,16},{2,18},{4,20},{6,22},{8,24},{10,26},{12,28},{14,30},{16,0},... | collective-permute-start | bytes 884744 | tf_op jit(solution)/shard_map/ppermute | solution.py:595
  28.7 30.8 %collective-permute-start.2 = (bf16[1,2,1,1,48,1536]{5,4,3,2,1,0:T(8,128)(2,1)S(1)}, bf16[1,2,1,1,48,1536]{5,4,3,2,1,0:T(8,128)(2,1)S(1)}, u32[]{:S(2)}, u32[]{:S(2)}) collective-permute-start(bf16[1,2,1,1,48,1536]{5,4,3,2,1,0:T(8,128)(2,1)S(1)} %pad_maximum_fusion.13), channel_id=1, source_target_pairs={{0,16},{2,18},{4,20},{6,22},{8,24},{10,26},{12,28},{14,30},{16,0},... | collective-permute-start | bytes 884744 | tf_op jit(solution)/shard_map/ppermute | solution.py:595
  29.3 35.3 %collective-permute-start.21 = (bf16[1,2,1,1,48,1536]{5,4,3,2,1,0:T(8,128)(2,1)S(1)}, bf16[1,2,1,1,48,1536]{5,4,3,2,1,0:T(8,128)(2,1)S(1)}, u32[]{:S(2)}, u32[]{:S(2)}) collective-permute-start(bf16[1,2,1,1,48,1536]{5,4,3,2,1,0:T(8,128)(2,1)S(1)} %pad_maximum_fusion.15), channel_id=1, source_target_pairs={{0,16},{2,18},{4,20},{6,22},{8,24},{10,26},{12,28},{14,30},{16,0},... | collective-permute-start | bytes 884744 | tf_op jit(solution)/shard_map/ppermute | solution.py:595
  53.3 23.4 %collective-permute-start.17 = (bf16[2,2,1,1,48,1536]{5,4,3,2,1,0:T(8,128)(2,1)S(1)}, bf16[2,2,1,1,48,1536]{5,4,3,2,1,0:T(8,128)(2,1)S(1)}, u32[]{:S(2)}, u32[]{:S(2)}) collective-permute-start(bf16[2,2,1,1,48,1536]{5,4,3,2,1,0:T(8,128)(2,1)S(1)} %pad_maximum_fusion.10), channel_id=1, source_target_pairs={{0,4},{2,6},{4,0},{6,2},{8,12},{10,14},{12,8},{14,10},{16,20},{18,... | collective-permute-start | bytes 1769480 | tf_op jit(solution)/shard_map/ppermute | solution.py:595
  60.1 15.8 %collective-permute-start.3 = (bf16[2,2,1,1,48,768]{5,4,3,2,1,0:T(8,128)(2,1)S(1)}, bf16[2,2,1,1,48,768]{5,4,3,2,1,0:T(8,128)(2,1)S(1)}, u32[]{:S(2)}, u32[]{:S(2)}) collective-permute-start(bf16[2,2,1,1,48,768]{5,4,3,2,1,0:T(8,128)(2,1)S(1)} %get-tuple-element.107), channel_id=1, source_target_pairs={{0,4},{2,6},{4,0},{6,2},{8,12},{10,14},{12,8},{14,10},{16,20},{18,... | collective-permute-start | bytes 884744 | tf_op jit(solution)/shard_map/ppermute | solution.py:595
  64.7 16.3 %collective-permute-start.22 = (bf16[2,2,1,1,48,1536]{5,4,3,2,1,0:T(8,128)(2,1)S(1)}, bf16[2,2,1,1,48,1536]{5,4,3,2,1,0:T(8,128)(2,1)S(1)}, u32[]{:S(2)}, u32[]{:S(2)}) collective-permute-start(bf16[2,2,1,1,48,1536]{5,4,3,2,1,0:T(8,128)(2,1)S(1)} %pad_maximum_fusion.11), channel_id=1, source_target_pairs={{0,1},{1,0},{2,3},{3,2},{4,5},{5,4},{6,7},{7,6},{8,9},{9,8},{10,11... | collective-permute-start | bytes 1769480 | tf_op jit(solution)/shard_map/ppermute | solution.py:594
  66.4 22.1 %collective-permute-start.7 = (bf16[2,2,1,1,48,1536]{5,4,3,2,1,0:T(8,128)(2,1)S(1)}, bf16[2,2,1,1,48,1536]{5,4,3,2,1,0:T(8,128)(2,1)S(1)}, u32[]{:S(2)}, u32[]{:S(2)}) collective-permute-start(bf16[2,2,1,1,48,1536]{5,4,3,2,1,0:T(8,128)(2,1)S(1)} %pad_maximum_fusion.9), channel_id=1, source_target_pairs={{0,4},{2,6},{4,0},{6,2},{8,12},{10,14},{12,8},{14,10},{16,20},{18,... | collective-permute-start | bytes 1769480 | tf_op jit(solution)/shard_map/ppermute | solution.py:595
  76.0 44.4 %collective-permute-start.4 = (bf16[2,2,2,1,48,768]{5,4,3,2,1,0:T(8,128)(2,1)S(1)}, bf16[2,2,2,1,48,768]{5,4,3,2,1,0:T(8,128)(2,1)S(1)}, u32[]{:S(2)}, u32[]{:S(2)}) collective-permute-start(bf16[2,2,2,1,48,768]{5,4,3,2,1,0:T(8,128)(2,1)S(1)} %pad_maximum_fusion.8), channel_id=1, source_target_pairs={{0,1},{1,0},{2,3},{3,2},{4,5},{5,4},{6,7},{7,6},{8,9},{9,8},{10,11... | collective-permute-start | bytes 1769480 | tf_op jit(solution)/shard_map/ppermute | solution.py:594
  76.8 40.1 %collective-permute-start.18 = (bf16[2,2,2,1,48,1536]{5,4,3,2,1,0:T(8,128)(2,1)S(1)}, bf16[2,2,2,1,48,1536]{5,4,3,2,1,0:T(8,128)(2,1)S(1)}, u32[]{:S(2)}, u32[]{:S(2)}) collective-permute-start(bf16[2,2,2,1,48,1536]{5,4,3,2,1,0:T(8,128)(2,1)S(1)} %pad_maximum_fusion.5), channel_id=1, source_target_pairs={{0,1},{1,0},{2,3},{3,2},{4,5},{5,4},{6,7},{7,6},{8,9},{9,8},{10,11... | collective-permute-start | bytes 3538952 | tf_op jit(solution)/shard_map/ppermute | solution.py:594
  81.3 36.2 %collective-permute-start.23 = (bf16[2,2,1,1,48,3072]{5,4,3,2,1,0:T(8,128)(2,1)S(1)}, bf16[2,2,1,1,48,3072]{5,4,3,2,1,0:T(8,128)(2,1)S(1)}, u32[]{:S(2)}, u32[]{:S(2)}) collective-permute-start(bf16[2,2,1,1,48,3072]{5,4,3,2,1,0:T(8,128)(2,1)S(1)} %pad_maximum_fusion.6), channel_id=1, source_target_pairs={{0,4},{2,6},{4,0},{6,2},{8,12},{10,14},{12,8},{14,10},{16,20},{18,... | collective-permute-start | bytes 3538952 | tf_op jit(solution)/shard_map/ppermute | solution.py:595
  88.9 58.1 %collective-permute-start.8 = (bf16[2,2,2,1,48,1536]{5,4,3,2,1,0:T(8,128)(2,1)S(1)}, bf16[2,2,2,1,48,1536]{5,4,3,2,1,0:T(8,128)(2,1)}, u32[]{:S(2)}, u32[]{:S(2)}) collective-permute-start(bf16[2,2,2,1,48,1536]{5,4,3,2,1,0:T(8,128)(2,1)S(1)} %pad_maximum_fusion.4), channel_id=1, source_target_pairs={{0,2},{2,0},{4,6},{6,4},{8,10},{10,8},{12,14},{14,12},{16,18},{18,... | collective-permute-start | bytes 3538952 | tf_op jit(solution)/shard_map/ppermute | solution.py:595
  117.4 41.4 %collective-permute-start.19 = (bf16[2,2,2,1,48,3072]{5,4,3,2,1,0:T(8,128)(2,1)S(1)}, bf16[2,2,2,1,48,3072]{5,4,3,2,1,0:T(8,128)(2,1)}, u32[]{:S(2)}, u32[]{:S(2)}) collective-permute-start(bf16[2,2,2,1,48,3072]{5,4,3,2,1,0:T(8,128)(2,1)S(1)} %pad_maximum_fusion), channel_id=1, source_target_pairs={{0,2},{2,0},{4,6},{6,4},{8,10},{10,8},{12,14},{14,12},{16,18},{18,... | collective-permute-start | bytes 7077896 | tf_op jit(solution)/shard_map/ppermute | solution.py:595
  120.4 53.4 %collective-permute-start.24 = (bf16[2,2,2,1,48,3072]{5,4,3,2,1,0:T(8,128)(2,1)}, bf16[2,2,2,1,48,3072]{5,4,3,2,1,0:T(8,128)(2,1)}, u32[]{:S(2)}, u32[]{:S(2)}) collective-permute-start(bf16[2,2,2,1,48,3072]{5,4,3,2,1,0:T(8,128)(2,1)} %pad_maximum_fusion.1), channel_id=1, source_target_pairs={{0,2},{2,0},{4,6},{6,4},{8,10},{10,8},{12,14},{14,12},{16,18},{18,... | collective-permute-start | bytes 7077896 | tf_op jit(solution)/shard_map/ppermute | solution.py:595
  121.7 25.3 %collective-permute-start.5 = (bf16[2,2,2,1,48,1536]{5,4,3,2,1,0:T(8,128)(2,1)}, bf16[2,2,2,1,48,1536]{5,4,3,2,1,0:T(8,128)(2,1)}, u32[]{:S(2)}, u32[]{:S(2)}) collective-permute-start(bf16[2,2,2,1,48,1536]{5,4,3,2,1,0:T(8,128)(2,1)} %pad_maximum_fusion.3), channel_id=1, source_target_pairs={{0,2},{2,0},{4,6},{6,4},{8,10},{10,8},{12,14},{14,12},{16,18},{18,... | collective-permute-start | bytes 3538952 | tf_op jit(solution)/shard_map/ppermute | solution.py:595
  127.4 16.7 %collective-permute-start = (bf16[2,128,768]{2,1,0:T(8,128)(2,1)}, bf16[2,128,768]{2,1,0:T(8,128)(2,1)}, u32[]{:S(2)}, u32[]{:S(2)}) collective-permute-start(bf16[2,128,768]{2,1,0:T(8,128)(2,1)} %get-tuple-element.98), channel_id=1, source_target_pairs={{0,1},{1,0},{2,3},{3,2},{4,5},{5,4},{6,7},{7,6},{8,9},{9,8},{10,11... | collective-permute-start | bytes 1179656 | tf_op jit(solution)/shard_map/ppermute | solution.py:594
  144.1 14.7 %collective-permute-start.14 = (bf16[2,128,768]{2,1,0:T(8,128)(2,1)}, bf16[2,128,768]{2,1,0:T(8,128)(2,1)S(1)}, u32[]{:S(2)}, u32[]{:S(2)}) collective-permute-start(bf16[2,128,768]{2,1,0:T(8,128)(2,1)} %get-tuple-element.96), channel_id=1, source_target_pairs={{0,1},{1,0},{2,3},{3,2},{4,5},{5,4},{6,7},{7,6},{8,9},{9,8},{10,11... | collective-permute-start | bytes 1179656 | tf_op jit(solution)/shard_map/ppermute | solution.py:594
  222.4 13.9 %collective-permute-start.35 = (bf16[8,48,1536]{2,1,0:T(8,128)(2,1)}, bf16[8,48,1536]{2,1,0:T(8,128)(2,1)S(1)}, u32[]{:S(2)}, u32[]{:S(2)}) collective-permute-start(bf16[8,48,1536]{2,1,0:T(8,128)(2,1)} %get-tuple-element.59), channel_id=1, source_target_pairs={{0,2},{2,0},{4,6},{6,4},{8,10},{10,8},{12,14},{14,12},{16,18},{18,... | collective-permute-start | bytes 3538952 | tf_op jit(solution)/shard_map/ppermute | solution.py:595
  231.3 57.6 %collective-permute-start.45 = (bf16[8,48,3072]{2,1,0:T(8,128)(2,1)}, bf16[8,48,3072]{2,1,0:T(8,128)(2,1)}, u32[]{:S(2)}, u32[]{:S(2)}) collective-permute-start(bf16[8,48,3072]{2,1,0:T(8,128)(2,1)} %get-tuple-element.63), channel_id=1, source_target_pairs={{0,2},{2,0},{4,6},{6,4},{8,10},{10,8},{12,14},{14,12},{16,18},{18,... | collective-permute-start | bytes 7077896 | tf_op jit(solution)/shard_map/ppermute | solution.py:595
  231.4 60.5 %collective-permute-start.40 = (bf16[8,48,3072]{2,1,0:T(8,128)(2,1)}, bf16[8,48,3072]{2,1,0:T(8,128)(2,1)S(1)}, u32[]{:S(2)}, u32[]{:S(2)}) collective-permute-start(bf16[8,48,3072]{2,1,0:T(8,128)(2,1)} %get-tuple-element.61), channel_id=1, source_target_pairs={{0,2},{2,0},{4,6},{6,4},{8,10},{10,8},{12,14},{14,12},{16,18},{18,... | collective-permute-start | bytes 7077896 | tf_op jit(solution)/shard_map/ppermute | solution.py:595
  235.8 34.2 %collective-permute-start.26 = (bf16[2,128,768]{2,1,0:T(8,128)(2,1)}, bf16[2,128,768]{2,1,0:T(8,128)(2,1)}, u32[]{:S(2)}, u32[]{:S(2)}) collective-permute-start(bf16[2,128,768]{2,1,0:T(8,128)(2,1)} %get-tuple-element.52), channel_id=1, source_target_pairs={{0,1},{1,0},{2,3},{3,2},{4,5},{5,4},{6,7},{7,6},{8,9},{9,8},{10,11... | collective-permute-start | bytes 1179656 | tf_op jit(solution)/shard_map/ppermute | solution.py:594
  240.4 14.4 %collective-permute-start.36 = (bf16[2,2,1,1,48,1536]{5,4,3,2,1,0:T(8,128)(2,1)}, bf16[2,2,1,1,48,1536]{5,4,3,2,1,0:T(8,128)(2,1)}, u32[]{:S(2)}, u32[]{:S(2)}) collective-permute-start(bf16[2,2,1,1,48,1536]{5,4,3,2,1,0:T(8,128)(2,1)} %constant_dynamic-slice_fusion.10), channel_id=1, source_target_pairs={{0,4},{2,6},{4,0},{6,2},{8,12},{10,14},{12,8},{14,10},{16,20},{18,... | collective-permute-start | bytes 1769480 | tf_op jit(solution)/shard_map/ppermute | solution.py:595
  243.7 33.3 %collective-permute-start.25 = (bf16[2,128,768]{2,1,0:T(8,128)(2,1)}, bf16[2,128,768]{2,1,0:T(8,128)(2,1)S(1)}, u32[]{:S(2)}, u32[]{:S(2)}) collective-permute-start(bf16[2,128,768]{2,1,0:T(8,128)(2,1)} %get-tuple-element.45), channel_id=1, source_target_pairs={{0,1},{1,0},{2,3},{3,2},{4,5},{5,4},{6,7},{7,6},{8,9},{9,8},{10,11... | collective-permute-start | bytes 1179656 | tf_op jit(solution)/shard_map/ppermute | solution.py:594
  254.8 13.5 %collective-permute-start.33 = (bf16[2,2,2,1,48,768]{5,4,3,2,1,0:T(8,128)(2,1)S(1)}, bf16[2,2,2,1,48,768]{5,4,3,2,1,0:T(8,128)(2,1)S(1)}, u32[]{:S(2)}, u32[]{:S(2)}) collective-permute-start(bf16[2,2,2,1,48,768]{5,4,3,2,1,0:T(8,128)(2,1)S(1)} %constant_dynamic-slice_fusion.12), channel_id=1, source_target_pairs={{0,1},{1,0},{2,3},{3,2},{4,5},{5,4},{6,7},{7,6},{8,9},{9,8},{10,11... | collective-permute-start | bytes 1769480 | tf_op jit(solution)/shard_map/ppermute | solution.py:594
  291.6 25.8 %collective-permute-start.46 = (bf16[2,2,2,1,48,1536]{5,4,3,2,1,0:T(8,128)(2,1)S(1)}, bf16[2,2,2,1,48,1536]{5,4,3,2,1,0:T(8,128)(2,1)S(1)}, u32[]{:S(2)}, u32[]{:S(2)}) collective-permute-start(bf16[2,2,2,1,48,1536]{5,4,3,2,1,0:T(8,128)(2,1)S(1)} %constant_dynamic-slice_fusion.3), channel_id=1, source_target_pairs={{0,1},{1,0},{2,3},{3,2},{4,5},{5,4},{6,7},{7,6},{8,9},{9,8},{10,11... | collective-permute-start | bytes 3538952 | tf_op jit(solution)/shard_map/ppermute | solution.py:594
  294.2 28.3 %collective-permute-start.41 = (bf16[2,2,1,1,48,3072]{5,4,3,2,1,0:T(8,128)(2,1)S(1)}, bf16[2,2,1,1,48,3072]{5,4,3,2,1,0:T(8,128)(2,1)S(1)}, u32[]{:S(2)}, u32[]{:S(2)}) collective-permute-start(bf16[2,2,1,1,48,3072]{5,4,3,2,1,0:T(8,128)(2,1)S(1)} %constant_dynamic-slice_fusion.7), channel_id=1, source_target_pairs={{0,4},{2,6},{4,0},{6,2},{8,12},{10,14},{12,8},{14,10},{16,20},{18,... | collective-permute-start | bytes 3538952 | tf_op jit(solution)/shard_map/ppermute | solution.py:595
  317.8 14.8 %collective-permute-start.47 = (bf16[2,2,1,1,48,1536]{5,4,3,2,1,0:T(8,128)(2,1)S(1)}, bf16[2,2,1,1,48,1536]{5,4,3,2,1,0:T(8,128)(2,1)S(1)}, u32[]{:S(2)}, u32[]{:S(2)}) collective-permute-start(bf16[2,2,1,1,48,1536]{5,4,3,2,1,0:T(8,128)(2,1)S(1)} %constant_dynamic-slice_fusion.2), channel_id=1, source_target_pairs={{0,4},{2,6},{4,0},{6,2},{8,12},{10,14},{12,8},{14,10},{16,20},{18,... | collective-permute-start | bytes 1769480 | tf_op jit(solution)/shard_map/ppermute | solution.py:595
  332.7 21.1 %collective-permute-start.48 = (bf16[1,2,1,1,48,1536]{5,4,3,2,1,0:T(8,128)(2,1)S(1)}, bf16[1,2,1,1,48,1536]{5,4,3,2,1,0:T(8,128)(2,1)S(1)}, u32[]{:S(2)}, u32[]{:S(2)}) collective-permute-start(bf16[1,2,1,1,48,1536]{5,4,3,2,1,0:T(8,128)(2,1)S(1)} %constant_dynamic-slice_fusion.1), channel_id=1, source_target_pairs={{0,16},{2,18},{4,20},{6,22},{8,24},{10,26},{12,28},{14,30},{16,0},... | collective-permute-start | bytes 884744 | tf_op jit(solution)/shard_map/ppermute | solution.py:595
  334.9 24.3 %collective-permute-start.43 = (bf16[1,2,1,1,48,1536]{5,4,3,2,1,0:T(8,128)(2,1)S(1)}, bf16[1,2,1,1,48,1536]{5,4,3,2,1,0:T(8,128)(2,1)S(1)}, u32[]{:S(2)}, u32[]{:S(2)}) collective-permute-start(bf16[1,2,1,1,48,1536]{5,4,3,2,1,0:T(8,128)(2,1)S(1)} %constant_dynamic-slice_fusion.5), channel_id=1, source_target_pairs={{0,16},{2,18},{4,20},{6,22},{8,24},{10,26},{12,28},{14,30},{16,0},... | collective-permute-start | bytes 884744 | tf_op jit(solution)/shard_map/ppermute | solution.py:595
  (38 other events, 279.3 us)
